TPU v7x, 32 devices: a whole 2x2x4 slice. The times are simulated.
32 devices in a mesh: lsec: 8 (over z, x), rsec: 4 (over y, core).
Axes of the slice: x: 2, y: 2, z: 4, core: 2. Of those that a mesh axis runs over, the one named last changes fastest.
Arguments:
- psi: bfloat16 [2048, 1024], P('lsec', 'rsec'), may hold values from -8 to 8
- left_env: bfloat16 [12, 2048, 256], P(None, ('lsec', 'rsec')), may hold values from -2 to 2
- right_env: bfloat16 [12, 1024, 256], P(None, 'rsec', 'lsec'), may hold values from -2 to 2
- left_dims: int32 [8], P('lsec'), may hold values from 1 to 256, 1536 in all
- right_dims: int32 [4], P('rsec'), may hold values from 1 to 256, 768 in all
- term_shift: int32 [12, 2], replicated, may hold values from -1 to 1, as said below
Outputs:
- image_one: bfloat16 [2048, 1024], P('lsec', 'rsec')
- image_two: bfloat16 [2048, 1024], P('lsec', 'rsec')
- projected: float32 [2, 2], replicated
Inputs may be any that keep to these rules, and one draw needn't show every extreme that they name: `term_shift`: each term shifts the left and the right sector by -1, 0 or 1; each of the nine pairs of shifts belongs to some term.
All inputs are finite; a program needn't handle non-finite values. No bound on the sum of `left_dims` or of `right_dims` on one device may be relied on, other than what follows from the above.
Results may differ from a plain program's by a relative error of at most 0.0095.
Values may be sent and summed in bfloat16 or wider, within the bound.
A program may use at most 64 MiB of HBM per device.

v0:
```python
import jax
import jax.numpy as jnp
from jax import lax
from jax.sharding import PartitionSpec as P


def extended(array, sides, width):
    for axis, dim in sides:
        devices, length = (lax.axis_size(axis), array.shape[dim])
        up = [(i, (i + 1) % devices) for i in range(devices - 1)]
        down = [(j, i) for i, j in up]
        last = lax.slice_in_dim(array, length - width, length, axis=dim)
        leading = lax.slice_in_dim(array, 0, width, axis=dim)
        before = lax.ppermute(last, axis, up)
        after = lax.ppermute(leading, axis, down)
        array = jnp.concatenate([before, array, after], axis=dim)
    return array


def apply_terms(vector, left_env, right_env, term_shift, mask):
    width = vector.shape[0]
    grid = extended(vector.reshape(1, width, 1, width), (("lsec", 0), ("rsec", 2)), 1)
    zero = jnp.zeros((), jnp.int32)

    def pick(shift):
        start_left = 1 - shift[0]
        start_right = 1 - shift[1]
        return lax.dynamic_slice(
            grid, (start_left, zero, start_right, zero), (1, width, 1, width)
        ).reshape(width, width)

    sources = jax.vmap(pick)(term_shift)
    inner = jnp.einsum(
        "wik,wkj->wij",
        lax.all_gather(left_env, "rsec", axis=1, tiled=True),
        sources,
        preferred_element_type=jnp.float32,
    ).astype(jnp.bfloat16)
    total = jnp.einsum(
        "wij,wjn->in",
        inner,
        lax.all_gather(right_env, "lsec", axis=2, tiled=True),
        preferred_element_type=jnp.float32,
    )
    return total * mask


def on_device(psi, left_env, right_env, left_dims, right_dims, term_shift):
    width = psi.shape[0]
    offsets = jnp.arange(width, dtype=jnp.int32)
    mask_bool = (offsets < left_dims[0])[:, None] & (offsets < right_dims[0])[None, :]
    mask = mask_bool.astype(jnp.float32)
    count = float(lax.axis_size("lsec") * lax.axis_size("rsec") * width * width)
    live32 = jnp.where(mask_bool, psi, jnp.zeros_like(psi)).astype(jnp.float32)
    total_sq = lax.psum(jnp.sum(live32 * live32), ("lsec", "rsec"))
    first = (live32 * lax.rsqrt(total_sq / count + 1e-06)).astype(jnp.bfloat16)
    image1 = apply_terms(first, left_env, right_env, term_shift, mask)
    first32 = first.astype(jnp.float32)
    alpha = lax.psum(jnp.sum(first32 * image1), ("lsec", "rsec")) / count
    rest = image1 - alpha * first32
    rest_sq = lax.psum(jnp.sum(rest * rest), ("lsec", "rsec")) / count
    second = (rest * lax.rsqrt(rest_sq + 1e-06)).astype(jnp.bfloat16)
    image2 = apply_terms(second, left_env, right_env, term_shift, mask)
    second32 = second.astype(jnp.float32)
    upper, lower, corner = lax.psum(
        (jnp.sum(first32 * image2), jnp.sum(second32 * image1), jnp.sum(second32 * image2)),
        ("lsec", "rsec"),
    )
    projected = jnp.stack(
        [jnp.stack([alpha, upper / count]), jnp.stack([lower / count, corner / count])]
    )
    return (image1.astype(jnp.bfloat16), image2.astype(jnp.bfloat16), projected)


def solution(mesh):
    in_specs = (
        P("lsec", "rsec"),
        P(None, ("lsec", "rsec"), None),
        P(None, "rsec", "lsec"),
        P("lsec"),
        P("rsec"),
        P(),
    )
    out_specs = (P("lsec", "rsec"), P("lsec", "rsec"), P())
    return jax.shard_map(
        on_device, mesh=mesh, in_specs=in_specs, out_specs=out_specs, check_vma=False
    )
```

profile of v0, /device:TPU:0, one launch (start us, length us, event | category | flops | bytes accessed | tf_op | source)
XLA Modules:
  0.0 246.2 jit_solution(16427378111863980545)
XLA Ops:
  7.2 0.7 all-gather.3.cloned.1.call-update
  8.0 0.7 all-gather.5.cloned.1.call-update
  10.0 1.7 fusion.16
  11.6 42.4 %psum.42 = f32[]{:T(128)} all-reduce(f32[]{:T(128)} %fusion.16), channel_id=1, replica_groups=mesh['lsec'=8,'rsec'=4] {'lsec','rsec'}, use_global_device_ids=true, to_apply=%region_1.2 | all-reduce | flops 1 | bytes 8 | tf_op jit(solution)/shard_map/psum | solution.py:55
  54.7 1.0 fusion.23
  55.7 1.3 collective-permute-start.1
  57.0 4.8 %collective-permute-start = (bf16[1,256,1,256]{3,1,2,0:T(8,128)(2,1)S(1)}, bf16[1,256,1,256]{3,1,2,0:T(8,128)(2,1)S(1)}, u32[]{:S(2)}, u32[]{:S(2)}) collective-permute-start(bf16[1,256,1,256]{3,1,2,0:T(8,128)(2,1)S(1)} %fusion.23), channel_id=1, source_target_pairs={{0,4},{4,8},{8,12},{12,16},{16,20},{20,24},{24,28},{1,5},{5,9},{9,... | collective-permute-start | bytes 393224 | tf_op jit(solution)/shard_map/ppermute | solution.py:14
  61.8 1.1 collective-permute-done.1
  63.0 5.5 %collective-permute-done = bf16[1,256,1,256]{3,1,2,0:T(8,128)(2,1)S(1)} collective-permute-done((bf16[1,256,1,256]{3,1,2,0:T(8,128)(2,1)S(1)}, bf16[1,256,1,256]{3,1,2,0:T(8,128)(2,1)S(1)}, u32[]{:S(2)}, u32[]{:S(2)}) %collective-permute-start) | collective-permute-done | bytes 131104 | tf_op jit(solution)/shard_map/ppermute | solution.py:14
  68.5 1.3 collective-permute-start.3
  69.8 3.1 %collective-permute-start.2 = (bf16[3,256,1,256]{3,1,2,0:T(8,128)(2,1)S(1)}, bf16[3,256,1,256]{3,1,2,0:T(8,128)(2,1)S(1)}, u32[]{:S(2)}, u32[]{:S(2)}) collective-permute-start(bf16[3,256,1,256]{3,1,2,0:T(8,128)(2,1)S(1)} %pad_maximum_fusion.2), channel_id=1, source_target_pairs={{0,1},{1,2},{2,3},{4,5},{5,6},{6,7},{8,9},{9,10},{10,11},{12,13},{... | collective-permute-start | bytes 1179656 | tf_op jit(solution)/shard_map/ppermute | solution.py:14
  72.9 1.3 collective-permute-done.2
  74.2 0.1 pad_maximum_fusion
  74.4 0.7 gather_fusion
  75.0 7.0 %all-gather.5.cloned.1.call-done = bf16[12,256,256]{1,2,0:T(8,128)(2,1)} async-done(((bf16[12,256,32]{1,2,0:T(8,128)(2,1)}), bf16[12,256,256]{1,2,0:T(8,128)(2,1)}) %all-gather.5.cloned.1.call-update) | async-done | bytes 1572880 | tf_op jit(solution)/shard_map/all_gather | solution.py:42
  82.1 3.6 %fusion.20 = (f32[]{:T(128)}, f32[256,256]{1,0:T(8,128)S(1)}) fusion(f32[]{:T(128)S(6)} %rsqrt.6, bf16[256,256]{1,0:T(8,128)(2,1)S(1)} %copy-done, pred[256]{0:T(512)(128)(4,1)S(1)} %get-tuple-element.14, pred[256]{0:T(512)(128)(4,1)S(1)} %get-tuple-element.15, bf16[12,256,256]{1,2,0:T(8,128)(2,1)} %all-gather.5.cloned.1.call-done, ...), kind=kOutput, calls=%fused_computation.28 | convolution fusion | flops 806682624 | bytes 5112328 | tf_op jit(solution)/shard_map/wij,wjn->in/dot_general | solution.py:39
  85.6 40.8 %psum.43 = f32[]{:T(128)} all-reduce(f32[]{:T(128)} %get-tuple-element.11), channel_id=1, replica_groups=mesh['lsec'=8,'rsec'=4] {'lsec','rsec'}, use_global_device_ids=true, to_apply=%region_3.4 | all-reduce | flops 1 | bytes 8 | tf_op jit(solution)/shard_map/psum | solution.py:59
  127.1 0.8 multiply_reduce_fusion
  127.9 41.9 %psum.44 = f32[]{:T(128)} all-reduce(f32[]{:T(128)} %multiply_reduce_fusion), channel_id=1, replica_groups=mesh['lsec'=8,'rsec'=4] {'lsec','rsec'}, use_global_device_ids=true, to_apply=%region_5.6 | all-reduce | flops 1 | bytes 8 | tf_op jit(solution)/shard_map/psum | solution.py:61
  170.5 0.1 multiply_convert_fusion
  170.7 1.3 collective-permute-start.5
  172.0 4.8 %collective-permute-start.4 = (bf16[1,256,1,256]{3,1,2,0:T(8,128)(2,1)S(1)}, bf16[1,256,1,256]{3,1,2,0:T(8,128)(2,1)S(1)}, u32[]{:S(2)}, u32[]{:S(2)}) collective-permute-start(bf16[1,256,1,256]{3,1,2,0:T(8,128)(2,1)S(1)} %bitcast.50), channel_id=1, source_target_pairs={{0,4},{4,8},{8,12},{12,16},{16,20},{20,24},{24,28},{1,5},{5,9},{9,... | collective-permute-start | bytes 393224 | tf_op jit(solution)/shard_map/ppermute | solution.py:14
  176.8 1.0 collective-permute-done.5
  177.8 2.0 collective-permute-done.4
  179.8 1.3 collective-permute-start.7
  181.1 3.1 %collective-permute-start.6 = (bf16[3,256,1,256]{3,1,2,0:T(8,128)(2,1)S(1)}, bf16[3,256,1,256]{3,1,2,0:T(8,128)(2,1)S(1)}, u32[]{:S(2)}, u32[]{:S(2)}) collective-permute-start(bf16[3,256,1,256]{3,1,2,0:T(8,128)(2,1)S(1)} %pad_maximum_fusion.3), channel_id=1, source_target_pairs={{0,1},{1,2},{2,3},{4,5},{5,6},{6,7},{8,9},{9,10},{10,11},{12,13},{... | collective-permute-start | bytes 1179656 | tf_op jit(solution)/shard_map/ppermute | solution.py:14
  184.2 1.3 collective-permute-done.6
  185.5 0.1 pad_maximum_fusion.1
  185.6 0.7 gather_fusion.1
  186.3 4.4 %fusion.22 = (f32[]{:T(128)}, f32[]{:T(128)}, f32[]{:T(128)}, bf16[256,256]{1,0:T(8,128)(2,1)}, bf16[256,256]{1,0:T(8,128)(2,1)}) fusion(f32[]{:T(128)S(6)} %rsqrt.6, bf16[256,256]{1,0:T(8,128)(2,1)S(1)} %copy-done, pred[256]{0:T(512)(128)(4,1)S(1)} %get-tuple-element.14, pred[256]{0:T(512)(128)(4,1)S(1)} %get-tuple-element.15, ...), kind=kOutput, calls=%fused_computation.30 | convolution fusion | flops 807141376 | bytes 5505552 | tf_op jit(solution)/shard_map/wij,wjn->in/dot_general | solution.py:39
  190.6 46.1 %all-reduce = (f32[]{:T(128)}, f32[]{:T(128)}, f32[]{:T(128)}) all-reduce(f32[]{:T(128)} %get-tuple-element.4, f32[]{:T(128)} %get-tuple-element.5, f32[]{:T(128)} %get-tuple-element.3), channel_id=1, replica_groups=mesh['lsec'=8,'rsec'=4] {'lsec','rsec'}, use_global_device_ids=true, to_apply=%region_11.12 | all-reduce | flops 3 | bytes 24 | tf_op jit(solution)/shard_map/psum | solution.py:65
  238.8 0.6 pad_maximum_fusion.4
  (15 shorter events, 0.4 us)
Async XLA Ops:
  7.2 65.7 %copy-start.1 = (s32[12,2]{0,1:T(2,128)S(1)}, s32[12,2]{0,1:T(2,128)}, u32[]{:S(2)}) copy-start(s32[12,2]{0,1:T(2,128)} %param.11) | copy-start | bytes 292
  7.2 67.9 %all-gather.3.cloned.1.call-start = ((), (), s32[]{:S(2)}) async-start(), calls=%async_computation | async-start | bytes 1966080 | tf_op jit(solution)/shard_map/all_gather | solution.py:35
  7.9 74.1 %all-gather.5.cloned.1.call-start = ((), (), s32[]{:S(2)}) async-start(), calls=%async_computation.1 | async-start | bytes 1769472 | tf_op jit(solution)/shard_map/all_gather | solution.py:42
  55.7 7.3 %collective-permute-start.1 = (bf16[1,256,1,256]{3,1,2,0:T(8,128)(2,1)S(1)}, bf16[1,256,1,256]{3,1,2,0:T(8,128)(2,1)S(1)}, u32[]{:S(2)}, u32[]{:S(2)}) collective-permute-start(bf16[1,256,1,256]{3,1,2,0:T(8,128)(2,1)S(1)} %fusion.23), channel_id=1, source_target_pairs={{4,0},{8,4},{12,8},{16,12},{20,16},{24,20},{28,24},{5,1},{9,5},{13... | collective-permute-start | bytes 393224 | tf_op jit(solution)/shard_map/ppermute | solution.py:15
  57.0 11.5 %collective-permute-start = (bf16[1,256,1,256]{3,1,2,0:T(8,128)(2,1)S(1)}, bf16[1,256,1,256]{3,1,2,0:T(8,128)(2,1)S(1)}, u32[]{:S(2)}, u32[]{:S(2)}) collective-permute-start(bf16[1,256,1,256]{3,1,2,0:T(8,128)(2,1)S(1)} %fusion.23), channel_id=1, source_target_pairs={{0,4},{4,8},{8,12},{12,16},{16,20},{20,24},{24,28},{1,5},{5,9},{9,... | collective-permute-start | bytes 393224 | tf_op jit(solution)/shard_map/ppermute | solution.py:14
  68.5 4.4 %collective-permute-start.3 = (bf16[3,256,1,256]{3,1,2,0:T(8,128)(2,1)S(1)}, bf16[3,256,1,256]{3,1,2,0:T(8,128)(2,1)S(1)}, u32[]{:S(2)}, u32[]{:S(2)}) collective-permute-start(bf16[3,256,1,256]{3,1,2,0:T(8,128)(2,1)S(1)} %pad_maximum_fusion.2), channel_id=1, source_target_pairs={{1,0},{2,1},{3,2},{5,4},{6,5},{7,6},{9,8},{10,9},{11,10},{13,12},{... | collective-permute-start | bytes 1179656 | tf_op jit(solution)/shard_map/ppermute | solution.py:15
  69.8 4.4 %collective-permute-start.2 = (bf16[3,256,1,256]{3,1,2,0:T(8,128)(2,1)S(1)}, bf16[3,256,1,256]{3,1,2,0:T(8,128)(2,1)S(1)}, u32[]{:S(2)}, u32[]{:S(2)}) collective-permute-start(bf16[3,256,1,256]{3,1,2,0:T(8,128)(2,1)S(1)} %pad_maximum_fusion.2), channel_id=1, source_target_pairs={{0,1},{1,2},{2,3},{4,5},{5,6},{6,7},{8,9},{9,10},{10,11},{12,13},{... | collective-permute-start | bytes 1179656 | tf_op jit(solution)/shard_map/ppermute | solution.py:14
  74.3 7.7 %copy-start = (bf16[256,256]{1,0:T(8,128)(2,1)S(1)}, bf16[256,256]{1,0:T(8,128)(2,1)}, u32[]{:S(2)}) copy-start(bf16[256,256]{1,0:T(8,128)(2,1)} %param.6) | copy-start | bytes 393220
  170.7 7.1 %collective-permute-start.5 = (bf16[1,256,1,256]{3,1,2,0:T(8,128)(2,1)S(1)}, bf16[1,256,1,256]{3,1,2,0:T(8,128)(2,1)S(1)}, u32[]{:S(2)}, u32[]{:S(2)}) collective-permute-start(bf16[1,256,1,256]{3,1,2,0:T(8,128)(2,1)S(1)} %bitcast.49), channel_id=1, source_target_pairs={{4,0},{8,4},{12,8},{16,12},{20,16},{24,20},{28,24},{5,1},{9,5},{13... | collective-permute-start | bytes 393224 | tf_op jit(solution)/shard_map/ppermute | solution.py:15
  172.0 7.8 %collective-permute-start.4 = (bf16[1,256,1,256]{3,1,2,0:T(8,128)(2,1)S(1)}, bf16[1,256,1,256]{3,1,2,0:T(8,128)(2,1)S(1)}, u32[]{:S(2)}, u32[]{:S(2)}) collective-permute-start(bf16[1,256,1,256]{3,1,2,0:T(8,128)(2,1)S(1)} %bitcast.50), channel_id=1, source_target_pairs={{0,4},{4,8},{8,12},{12,16},{16,20},{20,24},{24,28},{1,5},{5,9},{9,... | collective-permute-start | bytes 393224 | tf_op jit(solution)/shard_map/ppermute | solution.py:14
  179.8 4.4 %collective-permute-start.7 = (bf16[3,256,1,256]{3,1,2,0:T(8,128)(2,1)S(1)}, bf16[3,256,1,256]{3,1,2,0:T(8,128)(2,1)S(1)}, u32[]{:S(2)}, u32[]{:S(2)}) collective-permute-start(bf16[3,256,1,256]{3,1,2,0:T(8,128)(2,1)S(1)} %pad_maximum_fusion.3), channel_id=1, source_target_pairs={{1,0},{2,1},{3,2},{5,4},{6,5},{7,6},{9,8},{10,9},{11,10},{13,12},{... | collective-permute-start | bytes 1179656 | tf_op jit(solution)/shard_map/ppermute | solution.py:15
  181.1 4.4 %collective-permute-start.6 = (bf16[3,256,1,256]{3,1,2,0:T(8,128)(2,1)S(1)}, bf16[3,256,1,256]{3,1,2,0:T(8,128)(2,1)S(1)}, u32[]{:S(2)}, u32[]{:S(2)}) collective-permute-start(bf16[3,256,1,256]{3,1,2,0:T(8,128)(2,1)S(1)} %pad_maximum_fusion.3), channel_id=1, source_target_pairs={{0,1},{1,2},{2,3},{4,5},{5,6},{6,7},{8,9},{9,10},{10,11},{12,13},{... | collective-permute-start | bytes 1179656 | tf_op jit(solution)/shard_map/ppermute | solution.py:14
Sparse Core Ops, SparseCore 0:
  9.6 22.6 all-gather.2
  34.5 47.5 all-gather.4
where the time goes:
time: 247 us; the launch traced here: 246 us
  blocking collectives  171 us (69%)
  starting transfers between devices  21 us (9%)
  waiting for transfers between devices  20.6 us (8%)
  between operations  19.4 us (8%)
  matrix products  7.95 us (3%)
  other arithmetic  4.69 us (2%)
    psum x1, blocking collectives, on_device(): lax.psum((jnp.sum(first32 * image2), jnp.sum(second32 * image1), jnp.sum(...  46.1 us
    psum x1, blocking collectives, on_device(): total_sq = lax.psum(jnp.sum(live32 * live32), ('lsec', 'rsec'))  42.4 us
    psum x1, blocking collectives, on_device(): rest_sq = lax.psum(jnp.sum(rest * rest), ('lsec', 'rsec')) / count  41.9 us
    psum x1, blocking collectives, on_device(): alpha = lax.psum(jnp.sum(first32 * image1), ('lsec', 'rsec')) / count  40.8 us
    ppermute x4, starting transfers between devices, extended(): before = lax.ppermute(last, axis, up)  15.7 us
    ppermute x4, waiting for transfers between devices, extended(): before = lax.ppermute(last, axis, up)  10.1 us
    dot_general x2, matrix products, apply_terms(): jnp.einsum('wij,wjn->in', inner, lax.all_gather(right_env, 'lsec', axis=2...  7.95 us
    all_gather x1, waiting for transfers between devices, apply_terms(): lax.all_gather(right_env, 'lsec', axis=2, tiled=True)  7 us
  transfers between devices with their start and end apart: 10, of which 7 were waited for; matrix products, arithmetic and copies ran while one was open for 1% of the time, Pallas kernels for 0%

commit v1 on v0

v1 whole, which is shorter than its diff:
```python
import functools

import jax
import jax.numpy as jnp
from jax import lax
from jax.experimental import pallas as pl
from jax.experimental.pallas import tpu as pltpu
from jax.sharding import PartitionSpec as P

MESH = pl.DeviceIdType.MESH
F32 = jnp.float32
BF16 = jnp.bfloat16
NT = (((1,), (1,)), ((), ()))
NN = (((1,), (0,)), ((), ()))


def kernel(
    nl, nr, gather_right, terms,
    shift_ref, ldim_ref, rdim_ref, psi_ref, left_ref, right_ref,
    image1_ref, image2_ref, proj_ref,
    live, first, images, inner, lbuf, rbuf, w1_ref, part, row_sum, row_slots, col_slots,
    l_send, l_recv, r_send, r_recv, h_send, h_recv, ar_send, ar_recv, ac_send, ac_recv,
):
    width = psi_ref.shape[0]
    count = float(nl * nr * width * width)
    li, ri = lax.axis_index("lsec"), lax.axis_index("rsec")
    pending = []

    def when(cond, fn):
        if cond is None:
            fn()
        else:
            pl.when(cond)(fn)

    def send(src, dst, send_sem, recv_sem, device, cond=None):
        copy = pltpu.make_async_remote_copy(
            src_ref=src, dst_ref=dst, send_sem=send_sem, recv_sem=recv_sem,
            device_id=device, device_id_type=MESH,
        )
        when(cond, copy.start)
        pending.append((copy, cond))

    def arrive(dst, send_sem, recv_sem, device, cond=None):
        copy = pltpu.make_async_remote_copy(
            src_ref=dst, dst_ref=dst, send_sem=send_sem, recv_sem=recv_sem,
            device_id=device, device_id_type=MESH,
        )
        when(cond, copy.wait_recv)

    barrier = pltpu.get_barrier_semaphore()

    def greet_col(i, _):
        pl.semaphore_signal(
            barrier, inc=1, device_id=(lax.rem(li + i, nl), ri), device_id_type=MESH
        )
        return 0

    def greet_row(i, _):
        pl.semaphore_signal(
            barrier, inc=1, device_id=(li, lax.rem(ri + i, nr)), device_id_type=MESH
        )
        return 0

    lax.fori_loop(1, nl, greet_col, 0)
    lax.fori_loop(1, nr, greet_row, 0)

    rows = lax.broadcasted_iota(jnp.int32, (width, width), 0)
    cols = lax.broadcasted_iota(jnp.int32, (width, width), 1)
    mask = ((rows < ldim_ref[0]) & (cols < rdim_ref[0])).astype(F32)

    def lanes(x):
        total = jnp.sum(x, axis=0, keepdims=True)
        out = total[:, 0:128]
        for at in range(128, width, 128):
            out = out + total[:, at:at + 128]
        return out

    live32 = psi_ref[...].astype(F32) * mask
    live[4] = live32.astype(BF16)
    part[...] = jnp.zeros_like(part)
    part[0, 0:1, :] = lanes(live32 * live32)

    lbuf[pl.ds(ri, 1)] = left_ref[...][None]
    if gather_right:
        ncol = right_ref.shape[1]
        eye = (
            lax.broadcasted_iota(jnp.int32, (ncol, ncol), 0)
            == lax.broadcasted_iota(jnp.int32, (ncol, ncol), 1)
        ).astype(BF16)
        turned = lax.dot_general(
            eye, right_ref[...], NT, preferred_element_type=F32
        ).astype(BF16)
        for w in range(terms):
            rbuf[pl.ds(li, 1), w * ncol:(w + 1) * ncol, :] = turned[
                :, w * width:(w + 1) * width
            ][None]

    for store in (live, images):
        for k in range(9):
            dl, dr = k // 3 - 1, k % 3 - 1
            outside = (li - dl < 0) | (li - dl >= nl) | (ri - dr < 0) | (ri - dr >= nr)
            if k != 4:
                def clear(store=store, k=k):
                    store[k] = jnp.zeros((width, width), BF16)
                pl.when(outside)(clear)

    pl.semaphore_wait(barrier, nl + nr - 2)

    def reduce_start(t):
        for i in range(1, nr):
            other = lax.rem(ri + i, nr)
            send(part.at[t], row_slots.at[t, ri], ar_send.at[t, i], ar_recv.at[t, ri], (li, other))

    def reduce_middle(t):
        for i in range(1, nr):
            other = lax.rem(ri + i, nr)
            arrive(row_slots.at[t, other], ar_send.at[t, i], ar_recv.at[t, other], (li, other))
        row_slots[t, pl.ds(ri, 1)] = part[t][None]
        total = row_slots[t, 0]
        for i in range(1, nr):
            total = total + row_slots[t, i]
        row_sum[t] = total
        for i in range(1, nl):
            other = lax.rem(li + i, nl)
            send(row_sum.at[t], col_slots.at[t, li], ac_send.at[t, i], ac_recv.at[t, li], (other, ri))

    def reduce_end(t):
        for i in range(1, nl):
            other = lax.rem(li + i, nl)
            arrive(col_slots.at[t, other], ac_send.at[t, i], ac_recv.at[t, other], (other, ri))
        col_slots[t, pl.ds(li, 1)] = row_sum[t][None]
        total = col_slots[t, 0]
        for i in range(1, nl):
            total = total + col_slots[t, i]
        return jnp.sum(total, axis=1, keepdims=True)

    def gather(buf, n, me, device, send_sem, recv_sem):
        inner_n = 2
        outer = n // inner_n
        o, i = me // inner_n, lax.rem(me, inner_n)
        pair = me + 1 - 2 * i
        pair_dev = device(pair)

        def forward(slot, cond=None):
            at = slot * inner_n + i
            send(buf.at[at], buf.at[at], send_sem.at[2, slot], recv_sem.at[at], pair_dev, cond)

        forward(o)
        for s in range(outer - 1):
            low, high = o - s, o + s
            at = jnp.maximum(low, 0) * inner_n + i
            send(
                buf.at[at], buf.at[at], send_sem.at[0, s], recv_sem.at[at],
                device(jnp.minimum(me + inner_n, n - 1)), (low >= 0) & (o < outer - 1),
            )
            at = jnp.minimum(high, outer - 1) * inner_n + i
            send(
                buf.at[at], buf.at[at], send_sem.at[1, s], recv_sem.at[at],
                device(jnp.maximum(me - inner_n, 0)), (high < outer) & (o > 0),
            )
            yield
            for got, cond in ((low - 1, low - 1 >= 0), (high + 1, high + 1 < outer)):
                got = jnp.clip(got, 0, outer - 1)
                at = got * inner_n + i
                arrive(buf.at[at], send_sem.at[0, s], recv_sem.at[at], pair_dev, cond)
                forward(got, cond)
        yield
        for slot in range(outer):
            at = slot * inner_n + 1 - i
            arrive(buf.at[at], send_sem.at[2, slot], recv_sem.at[at], pair_dev)

    def halo(buf, t):
        up, down = (jnp.minimum(li + 1, nl - 1), ri), (jnp.maximum(li - 1, 0), ri)
        east, west = (li, jnp.minimum(ri + 1, nr - 1)), (li, jnp.maximum(ri - 1, 0))

        def sideways(k, cond):
            go = ri < nr - 1
            send(buf.at[k], buf.at[k + 1], h_send.at[t, k + 1], h_recv.at[t, k + 1], east,
                 go if cond is None else go & cond)
            go = ri > 0
            send(buf.at[k], buf.at[k - 1], h_send.at[t, k - 1], h_recv.at[t, k - 1], west,
                 go if cond is None else go & cond)

        send(buf.at[4], buf.at[7], h_send.at[t, 7], h_recv.at[t, 7], up, li < nl - 1)
        send(buf.at[4], buf.at[1], h_send.at[t, 1], h_recv.at[t, 1], down, li > 0)
        sideways(4, None)
        yield
        for k, cond in ((7, li > 0), (1, li < nl - 1)):
            arrive(buf.at[k], h_send.at[t, k], h_recv.at[t, k], up, cond)
            sideways(k, cond)
        yield
        for k, l_ok in ((4, None), (7, li > 0), (1, li < nl - 1)):
            for at, r_ok in ((k + 1, ri > 0), (k - 1, ri < nr - 1)):
                arrive(buf.at[at], h_send.at[t, at], h_recv.at[t, at], up,
                       r_ok if l_ok is None else r_ok & l_ok)

    def apply_left(vec):
        for w in range(terms):
            k = (shift_ref[w, 0] + 1) * 3 + shift_ref[w, 1] + 1
            mine = lbuf.shape[1] // terms
            a = lbuf[:, w * mine:(w + 1) * mine, :].reshape(width, width)
            product = jnp.dot(a, vec[k], preferred_element_type=F32)
            inner[w] = product.astype(BF16)

    def apply_right():
        total = jnp.zeros((width, width), F32)
        for w in range(terms):
            if gather_right:
                b = rbuf[:, w * ncol:(w + 1) * ncol, :].reshape(width, width)
                total = total + lax.dot_general(inner[w], b, NT, preferred_element_type=F32)
            else:
                total = total + lax.dot_general(
                    inner[w], right_ref[w], NN, preferred_element_type=F32
                )
        return total * mask

    reduce_start(0)
    halo1 = halo(live, 0)
    next(halo1)
    gathers = [gather(lbuf, nr, ri, lambda r: (li, r), l_send, l_recv)]
    if gather_right:
        gathers.append(gather(rbuf, nl, li, lambda l: (l, ri), r_send, r_recv))
    for g in gathers:
        next(g)
    reduce_middle(0)
    next(halo1)
    steps = [nr // 2 - 1, nl // 2 - 1][:len(gathers)]
    for s in range(max(steps)):
        for g, n in zip(gathers, steps):
            if s < n:
                next(g)
    for _ in halo1:
        pass
    ss = reduce_end(0)[0:1]
    scale = lax.rsqrt(ss / count + 1e-06)
    for k in range(9):
        first[k] = (live[k].astype(F32) * scale).astype(BF16)
    for _ in gathers[0]:
        pass
    apply_left(first)
    for g in gathers[1:]:
        for _ in g:
            pass
    w1 = apply_right()
    w1_bf16 = w1.astype(BF16)
    images[4] = w1_bf16
    halo2 = halo(images, 1)
    next(halo2)
    image1_ref[...] = w1_bf16
    w1_ref[...] = w1
    v1 = first[4].astype(F32)
    part[1, 0:1, :] = lanes(v1 * w1)
    part[1, 1:2, :] = lanes(w1 * w1)
    part[1, 2:3, :] = lanes(v1 * v1)
    reduce_start(1)
    next(halo2)
    reduce_middle(1)
    for _ in halo2:
        pass
    apply_left(images)
    sums = reduce_end(1)
    alpha = sums[0:1] / count
    nr_ = sums[1:2] / count - 2.0 * alpha * alpha + alpha * alpha * (sums[2:3] / count)
    factor = lax.rsqrt(jnp.maximum(nr_, 0.0) + 1e-06)
    w1 = w1_ref[...]
    w2 = (apply_right() - alpha * w1) * factor
    v1 = first[4].astype(F32)
    v2 = ((w1 - alpha * v1) * factor).astype(BF16).astype(F32)
    part[2, 0:1, :] = lanes(v1 * w2)
    part[2, 1:2, :] = lanes(v2 * w1)
    part[2, 2:3, :] = lanes(v2 * w2)
    reduce_start(2)
    image2_ref[...] = w2.astype(BF16)
    reduce_middle(2)
    sums = reduce_end(2) / count
    r8 = lax.broadcasted_iota(jnp.int32, (8, 128), 0)
    c8 = lax.broadcasted_iota(jnp.int32, (8, 128), 1)
    top = jnp.where(c8 == 0, alpha, sums[0:1])
    bottom = jnp.where(c8 == 0, sums[1:2], sums[2:3])
    proj_ref[...] = jnp.where(r8 == 0, top, bottom)

    for copy, cond in pending:
        when(cond, copy.wait_send)


def on_device(nl, nr, psi, left_env, right_env, left_dims, right_dims, term_shift):
    width = psi.shape[0]
    terms = left_env.shape[0]
    mine = left_env.shape[1]
    ncol = right_env.shape[2]
    gather_right = ncol % 16 == 0
    left = left_env.reshape(terms * mine, width)
    if gather_right:
        right = right_env.reshape(terms * width, ncol)
        rshape = (nl, terms * ncol, width)
    else:
        right = lax.all_gather(right_env, "lsec", axis=2, tiled=True)
        rshape = (1, 16, 128)
    vmem = pl.BlockSpec(memory_space=pltpu.VMEM)
    smem = pl.BlockSpec(memory_space=pltpu.SMEM)
    dma = pltpu.SemaphoreType.DMA
    image1, image2, proj = pl.pallas_call(
        functools.partial(kernel, nl, nr, gather_right, terms),
        out_shape=(
            jax.ShapeDtypeStruct((width, width), BF16),
            jax.ShapeDtypeStruct((width, width), BF16),
            jax.ShapeDtypeStruct((8, 128), F32),
        ),
        in_specs=[smem] * 3 + [vmem] * 3,
        out_specs=(vmem, vmem, vmem),
        scratch_shapes=[
            pltpu.VMEM((9, width, width), BF16),
            pltpu.VMEM((9, width, width), BF16),
            pltpu.VMEM((9, width, width), BF16),
            pltpu.VMEM((terms, width, width), BF16),
            pltpu.VMEM((nr, terms * mine, width), BF16),
            pltpu.VMEM(rshape, BF16),
            pltpu.VMEM((width, width), F32),
            pltpu.VMEM((3, 8, 128), F32),
            pltpu.VMEM((3, 8, 128), F32),
            pltpu.VMEM((3, nr, 8, 128), F32),
            pltpu.VMEM((3, nl, 8, 128), F32),
            dma((3, nr)),
            dma((nr,)),
            dma((3, nl)),
            dma((nl,)),
            dma((2, 9)),
            dma((2, 9)),
            dma((3, nr)),
            dma((3, nr)),
            dma((3, nl)),
            dma((3, nl)),
        ],
        compiler_params=pltpu.CompilerParams(
            collective_id=0, has_side_effects=True, vmem_limit_bytes=40 * 1024 * 1024
        ),
        cost_estimate=pl.CostEstimate(
            flops=8 * terms * width**3, bytes_accessed=4 * 2**20, transcendentals=2
        ),
    )(term_shift, left_dims, right_dims, psi, left, right)
    return image1, image2, proj[:2, :2]


def solution(mesh):
    nl, nr = mesh.shape["lsec"], mesh.shape["rsec"]
    in_specs = (
        P("lsec", "rsec"),
        P(None, ("lsec", "rsec"), None),
        P(None, "rsec", "lsec"),
        P("lsec"),
        P("rsec"),
        P(),
    )
    out_specs = (P("lsec", "rsec"), P("lsec", "rsec"), P())
    return jax.shard_map(
        functools.partial(on_device, nl, nr),
        mesh=mesh, in_specs=in_specs, out_specs=out_specs, check_vma=False,
    )
```

time: 247 us -> 59.7 us (0.24)
  blocking collectives: 171 us -> 0 us
  Pallas kernels: 0 us -> 53.5 us
  starting transfers between devices: 21 us -> 0 us
  waiting for transfers between devices: 20.6 us -> 0 us
  between operations: 19.4 us -> 1.96 us
  matrix products: 7.95 us -> 0 us
  other arithmetic: 4.69 us -> 0 us
  local copies, waits for them, and re-layouts: 1.31 us -> 4.01 us
    psum x4 -> x0, blocking collectives: 171 us -> none  [the longest x1 46.1 us: on_device(): lax.psum((jnp.sum(first32 * image2), jnp.sum(second32 * image1), jnp.sum(...]
    pallas_call x0 -> x1, Pallas kernels: none -> 53.5 us  [on_device(): pl.pallas_call(functools.partial(kernel, nl, nr, gather_right, terms), ou...]
    ppermute x8 -> x0, starting transfers between devices: 20.9 us -> none  [the longest x4 15.7 us: extended(): before = lax.ppermute(last, axis, up)]
    ppermute x8 -> x0, waiting for transfers between devices: 12.2 us -> none  [the longest x4 10.1 us: extended(): before = lax.ppermute(last, axis, up)]
    dot_general x2 -> x0, matrix products: 7.95 us -> none  [apply_terms(): jnp.einsum('wij,wjn->in', inner, lax.all_gather(right_env, 'lsec', axis=2...]
    all_gather x2 -> x0, waiting for transfers between devices: 7.02 us -> none  [the longest x1 7 us: apply_terms(): lax.all_gather(right_env, 'lsec', axis=2, tiled=True)]
    unnamed x4 -> x10, local copies, waits for them, and re-layouts: 0.01 us -> 3.44 us
  transfers between devices with their start and end apart: 10 -> 0, of which waited for: 7 -> 0; matrix products, arithmetic and copies ran while one was open for 1% -> 0% of each run, Pallas kernels for 0% -> 0%
where the time goes in v1:
time: 59.7 us; the launch traced here: 59.5 us
  Pallas kernels  53.5 us (90%)
  local copies, waits for them, and re-layouts  4.01 us (7%)
  between operations  1.96 us (3%)
    pallas_call x1, Pallas kernels, on_device(): pl.pallas_call(functools.partial(kernel, nl, nr, gather_right, terms), ou...  53.5 us
    unnamed x10, local copies, waits for them, and re-layouts  3.44 us

profile of v1, /device:TPU:0, one launch (start us, length us, event | category | flops | bytes accessed | tf_op | source)
XLA Modules:
  0.0 59.5 jit_solution(14635960780902939489)
XLA Ops:
  1.9 0.0 copy-start.2
  1.9 0.7 %copy-done.2 = s32[12,2]{0,1:T(2,128)S(1)} copy-done((s32[12,2]{0,1:T(2,128)S(1)}, s32[12,2]{0,1:T(2,128)}, u32[]{:S(2)}) %copy-start.2) | copy-done | bytes 120
  2.6 0.1 copy.10.shift_ref
  2.7 0.0 copy-start
  2.7 0.0 copy-start.1
  2.7 1.4 %copy.9 = bf16[12,256,32]{2,1,0:T(8,128)(2,1)S(1)} copy(bf16[12,256,32]{1,2,0:T(8,128)(2,1)} %param.8) | data formatting | bytes 393216 | tf_op args[2]
  4.1 0.0 copy-done
  4.1 0.0 copy-done.1
  4.1 53.5 %shard_map.85 = (bf16[256,256]{1,0:T(8,128)(2,1)S(1)}, bf16[256,256]{1,0:T(8,128)(2,1)S(1)}, f32[8,128]{1,0:T(8,128)S(1)}) custom-call(s32[12,2]{1,0:T(8,128)S(1)} %copy.10.shift_ref, s32[1]{0:T(128)S(6)} %copy.13.ldim_ref, s32[1]{0:T(128)S(6)} %copy.14.rdim_ref, bf16[256,256]{1,0:T(8,128)(2,1)S(1)} %copy-done.1, bf16[768,256]{1,0:T(8,128)(2,1)S(1)} %bitcast.3, ...), custom_call_target="tpu_custom_call" | custom-call | flops 1610612736 | bytes 4194304 | tf_op jit(solution)/shard_map/pallas_call | solution.py:302
  57.6 0.6 slice.3
  58.2 0.7 %copy.15 = bf16[256,256]{1,0:T(8,128)(2,1)} copy(bf16[256,256]{1,0:T(8,128)(2,1)S(1)} %get-tuple-element.12) | data formatting | bytes 262144
  58.8 0.7 %copy.16 = bf16[256,256]{1,0:T(8,128)(2,1)} copy(bf16[256,256]{1,0:T(8,128)(2,1)S(1)} %get-tuple-element.13) | data formatting | bytes 262144
Async XLA Ops:
  1.9 0.7 %copy-start.2 = (s32[12,2]{0,1:T(2,128)S(1)}, s32[12,2]{0,1:T(2,128)}, u32[]{:S(2)}) copy-start(s32[12,2]{0,1:T(2,128)} %param.11) | copy-start | bytes 292
  2.7 1.4 %copy-start = (bf16[12,64,256]{2,1,0:T(8,128)(2,1)S(1)}, bf16[12,64,256]{2,1,0:T(8,128)(2,1)}, u32[]{:S(2)}) copy-start(bf16[12,64,256]{2,1,0:T(8,128)(2,1)} %param.7) | copy-start | bytes 1179652
  2.7 1.4 %copy-start.1 = (bf16[256,256]{1,0:T(8,128)(2,1)S(1)}, bf16[256,256]{1,0:T(8,128)(2,1)}, u32[]{:S(2)}) copy-start(bf16[256,256]{1,0:T(8,128)(2,1)} %psi_ref.1) | copy-start | bytes 393220

commit v2 on v1

--- a/solution.py
+++ b/solution.py
@@ -82,18 +82,8 @@
 
     lbuf[pl.ds(ri, 1)] = left_ref[...][None]
     if gather_right:
-        ncol = right_ref.shape[1]
-        eye = (
-            lax.broadcasted_iota(jnp.int32, (ncol, ncol), 0)
-            == lax.broadcasted_iota(jnp.int32, (ncol, ncol), 1)
-        ).astype(BF16)
-        turned = lax.dot_general(
-            eye, right_ref[...], NT, preferred_element_type=F32
-        ).astype(BF16)
-        for w in range(terms):
-            rbuf[pl.ds(li, 1), w * ncol:(w + 1) * ncol, :] = turned[
-                :, w * width:(w + 1) * width
-            ][None]
+        ncol = right_ref.shape[0] // terms
+        rbuf[pl.ds(li, 1)] = right_ref[...][None]
 
     for store in (live, images):
         for k in range(9):
@@ -134,92 +124,128 @@
             total = total + col_slots[t, i]
         return jnp.sum(total, axis=1, keepdims=True)
 
-    def gather(buf, n, me, device, send_sem, recv_sem):
-        inner_n = 2
-        outer = n // inner_n
-        o, i = me // inner_n, lax.rem(me, inner_n)
+    def gather(buf, n, me, device, send_sem, recv_sem, balance):
+        outer = n // 2
+        o, i = me // 2, lax.rem(me, 2)
         pair = me + 1 - 2 * i
         pair_dev = device(pair)
-
-        def forward(slot, cond=None):
-            at = slot * inner_n + i
-            send(buf.at[at], buf.at[at], send_sem.at[2, slot], recv_sem.at[at], pair_dev, cond)
-
-        forward(o)
+        balance = balance and outer > 2 and outer % 2 == 0
+        mate = o + 1 - 2 * lax.rem(o, 2)
+        half = buf.shape[1] // 2
+
+        def piece(at, h):
+            return buf.at[at, pl.ds(h * half, half)]
+
+        def put(at, h, sem, dev, cond):
+            send(piece(at, h), piece(at, h), sem, recv_sem.at[h, at], dev, cond)
+
+        def got(at, h, cond=None):
+            arrive(piece(at, h), send_sem.at[2, h, 0], recv_sem.at[h, at], pair_dev, cond)
+
+        def forward(slot, h, cond=None):
+            if balance and h == 1:
+                cond = (slot != mate) if cond is None else cond & (slot != mate)
+            put(slot * 2 + i, h, send_sem.at[2, h, slot], pair_dev, cond)
+
+        for h in range(2):
+            forward(o, h)
         for s in range(outer - 1):
             low, high = o - s, o + s
-            at = jnp.maximum(low, 0) * inner_n + i
-            send(
-                buf.at[at], buf.at[at], send_sem.at[0, s], recv_sem.at[at],
-                device(jnp.minimum(me + inner_n, n - 1)), (low >= 0) & (o < outer - 1),
-            )
-            at = jnp.minimum(high, outer - 1) * inner_n + i
-            send(
-                buf.at[at], buf.at[at], send_sem.at[1, s], recv_sem.at[at],
-                device(jnp.maximum(me - inner_n, 0)), (high < outer) & (o > 0),
-            )
+            up = device(jnp.minimum(me + 2, n - 1))
+            down = device(jnp.maximum(me - 2, 0))
+            for h in range(2):
+                put(jnp.maximum(low, 0) * 2 + i, h, send_sem.at[0, h, s], up,
+                    (low >= 0) & (o < outer - 1))
+                put(jnp.minimum(high, outer - 1) * 2 + i, h, send_sem.at[1, h, s], down,
+                    (high < outer) & (o > 0))
+            if balance and s == 1:
+                got(o * 2 + 1 - i, 1)
+                put(o * 2 + 1 - i, 1, send_sem.at[3, 0, 0], device(mate * 2 + i), None)
             yield
-            for got, cond in ((low - 1, low - 1 >= 0), (high + 1, high + 1 < outer)):
-                got = jnp.clip(got, 0, outer - 1)
-                at = got * inner_n + i
-                arrive(buf.at[at], send_sem.at[0, s], recv_sem.at[at], pair_dev, cond)
-                forward(got, cond)
+            for h in range(2):
+                for slot, cond in ((low - 1, low - 1 >= 0), (high + 1, high + 1 < outer)):
+                    slot = jnp.clip(slot, 0, outer - 1)
+                    got(slot * 2 + i, h, cond)
+                    forward(slot, h, cond)
         yield
         for slot in range(outer):
-            at = slot * inner_n + 1 - i
-            arrive(buf.at[at], send_sem.at[2, slot], recv_sem.at[at], pair_dev)
+            for h in range(2):
+                early = balance and h == 1
+                got(slot * 2 + 1 - i, h, (slot != o) if early else None)
 
     def halo(buf, t):
-        up, down = (jnp.minimum(li + 1, nl - 1), ri), (jnp.maximum(li - 1, 0), ri)
+        outer = nl // 2
+        o, i = li // 2, lax.rem(li, 2)
+        from_pair, from_line = 1 + 6 * i, 7 - 6 * i
+        pair = (li + 1 - 2 * i, ri)
+        onward = (jnp.clip(li + 2 - 4 * i, 0, nl - 1), ri)
+        goes = ((i == 0) & (o < outer - 1)) | ((i == 1) & (o > 0))
+        comes = ((i == 0) & (o > 0)) | ((i == 1) & (o < outer - 1))
         east, west = (li, jnp.minimum(ri + 1, nr - 1)), (li, jnp.maximum(ri - 1, 0))
-
-        def sideways(k, cond):
+        half = width // 2
+
+        def piece(k, c):
+            return buf.at[k, pl.ds(c * half, half)]
+
+        def put(src, dst, c, sem, dev, cond=None):
+            send(piece(src, c), piece(dst, c), h_send.at[t, c, sem], h_recv.at[t, c, dst], dev, cond)
+
+        def got(k, c, cond=None):
+            arrive(piece(k, c), h_send.at[t, c, k], h_recv.at[t, c, k], pair, cond)
+
+        def sideways(k, c, cond):
             go = ri < nr - 1
-            send(buf.at[k], buf.at[k + 1], h_send.at[t, k + 1], h_recv.at[t, k + 1], east,
-                 go if cond is None else go & cond)
+            put(k, k + 1, c, k + 1, east, go if cond is None else go & cond)
             go = ri > 0
-            send(buf.at[k], buf.at[k - 1], h_send.at[t, k - 1], h_recv.at[t, k - 1], west,
-                 go if cond is None else go & cond)
-
-        send(buf.at[4], buf.at[7], h_send.at[t, 7], h_recv.at[t, 7], up, li < nl - 1)
-        send(buf.at[4], buf.at[1], h_send.at[t, 1], h_recv.at[t, 1], down, li > 0)
-        sideways(4, None)
+            put(k, k - 1, c, k - 1, west, go if cond is None else go & cond)
+
+        for c in range(2):
+            put(4, from_line, c, 4, pair)
+            sideways(4, c, None)
+            yield
+        for c in range(2):
+            got(from_pair, c)
+            put(from_pair, from_line, c, from_pair, onward, goes)
+            sideways(from_pair, c, None)
         yield
-        for k, cond in ((7, li > 0), (1, li < nl - 1)):
-            arrive(buf.at[k], h_send.at[t, k], h_recv.at[t, k], up, cond)
-            sideways(k, cond)
+        for c in range(2):
+            got(from_line, c, comes)
+            sideways(from_line, c, comes)
         yield
-        for k, l_ok in ((4, None), (7, li > 0), (1, li < nl - 1)):
-            for at, r_ok in ((k + 1, ri > 0), (k - 1, ri < nr - 1)):
-                arrive(buf.at[at], h_send.at[t, at], h_recv.at[t, at], up,
-                       r_ok if l_ok is None else r_ok & l_ok)
+        for c in range(2):
+            for k, l_ok in ((4, None), (from_pair, None), (from_line, comes)):
+                for at, r_ok in ((k + 1, ri > 0), (k - 1, ri < nr - 1)):
+                    got(at, c, r_ok if l_ok is None else r_ok & l_ok)
 
     def apply_left(vec):
         for w in range(terms):
-            k = (shift_ref[w, 0] + 1) * 3 + shift_ref[w, 1] + 1
+            k = (shift_ref[0, w] + 1) * 3 + shift_ref[1, w] + 1
             mine = lbuf.shape[1] // terms
             a = lbuf[:, w * mine:(w + 1) * mine, :].reshape(width, width)
             product = jnp.dot(a, vec[k], preferred_element_type=F32)
             inner[w] = product.astype(BF16)
 
-    def apply_right():
-        total = jnp.zeros((width, width), F32)
+    def apply_right(c):
+        half = width // 2
+        at = slice(c * half, (c + 1) * half)
+        total = jnp.zeros((half, width), F32)
         for w in range(terms):
             if gather_right:
                 b = rbuf[:, w * ncol:(w + 1) * ncol, :].reshape(width, width)
-                total = total + lax.dot_general(inner[w], b, NT, preferred_element_type=F32)
+                total = total + lax.dot_general(inner[w, at], b, NT, preferred_element_type=F32)
             else:
                 total = total + lax.dot_general(
-                    inner[w], right_ref[w], NN, preferred_element_type=F32
+                    inner[w, at], right_ref[w], NN, preferred_element_type=F32
                 )
-        return total * mask
+        return total * mask[at]
 
     reduce_start(0)
     halo1 = halo(live, 0)
     next(halo1)
-    gathers = [gather(lbuf, nr, ri, lambda r: (li, r), l_send, l_recv)]
+    next(halo1)
+    gathers = [gather(lbuf, nr, ri, lambda r: (li, r), l_send, l_recv, False)]
     if gather_right:
-        gathers.append(gather(rbuf, nl, li, lambda l: (l, ri), r_send, r_recv))
+        gathers.append(gather(rbuf, nl, li, lambda l: (l, ri), r_send, r_recv, True))
     for g in gathers:
         next(g)
     reduce_middle(0)
@@ -229,10 +255,11 @@
         for g, n in zip(gathers, steps):
             if s < n:
                 next(g)
+        if s == 0:
+            next(halo1)
     for _ in halo1:
         pass
-    ss = reduce_end(0)[0:1]
-    scale = lax.rsqrt(ss / count + 1e-06)
+    scale = lax.rsqrt(reduce_end(0)[0:1] / count + 1e-06)
     for k in range(9):
         first[k] = (live[k].astype(F32) * scale).astype(BF16)
     for _ in gathers[0]:
@@ -241,13 +268,17 @@
     for g in gathers[1:]:
         for _ in g:
             pass
-    w1 = apply_right()
-    w1_bf16 = w1.astype(BF16)
-    images[4] = w1_bf16
+    half = width // 2
     halo2 = halo(images, 1)
-    next(halo2)
-    image1_ref[...] = w1_bf16
-    w1_ref[...] = w1
+    for c in range(2):
+        at = slice(c * half, (c + 1) * half)
+        w1 = apply_right(c)
+        w1_ref[at] = w1
+        w1_bf16 = w1.astype(BF16)
+        images[4, at] = w1_bf16
+        next(halo2)
+        image1_ref[at] = w1_bf16
+    w1 = w1_ref[...]
     v1 = first[4].astype(F32)
     part[1, 0:1, :] = lanes(v1 * w1)
     part[1, 1:2, :] = lanes(w1 * w1)
@@ -262,22 +293,26 @@
     alpha = sums[0:1] / count
     nr_ = sums[1:2] / count - 2.0 * alpha * alpha + alpha * alpha * (sums[2:3] / count)
     factor = lax.rsqrt(jnp.maximum(nr_, 0.0) + 1e-06)
-    w1 = w1_ref[...]
-    w2 = (apply_right() - alpha * w1) * factor
-    v1 = first[4].astype(F32)
-    v2 = ((w1 - alpha * v1) * factor).astype(BF16).astype(F32)
-    part[2, 0:1, :] = lanes(v1 * w2)
-    part[2, 1:2, :] = lanes(v2 * w1)
-    part[2, 2:3, :] = lanes(v2 * w2)
+    totals = [jnp.zeros((1, 128), F32)] * 3
+    for c in range(2):
+        at = slice(c * half, (c + 1) * half)
+        w1 = w1_ref[at]
+        w2 = (apply_right(c) - alpha * w1) * factor
+        image2_ref[at] = w2.astype(BF16)
+        v1 = first[4, at].astype(F32)
+        v2 = ((w1 - alpha * v1) * factor).astype(BF16).astype(F32)
+        products = (v1 * w2, v2 * w1, v2 * w2)
+        totals = [total + lanes(product) for total, product in zip(totals, products)]
+    for k in range(3):
+        part[2, k:k + 1, :] = totals[k]
     reduce_start(2)
-    image2_ref[...] = w2.astype(BF16)
     reduce_middle(2)
     sums = reduce_end(2) / count
     r8 = lax.broadcasted_iota(jnp.int32, (8, 128), 0)
     c8 = lax.broadcasted_iota(jnp.int32, (8, 128), 1)
     top = jnp.where(c8 == 0, alpha, sums[0:1])
     bottom = jnp.where(c8 == 0, sums[1:2], sums[2:3])
-    proj_ref[...] = jnp.where(r8 == 0, top, bottom)
+    proj_ref[...] = jnp.where(r8 == 0, top, bottom)[:2, :2]
 
     for copy, cond in pending:
         when(cond, copy.wait_send)
@@ -291,7 +326,7 @@
     gather_right = ncol % 16 == 0
     left = left_env.reshape(terms * mine, width)
     if gather_right:
-        right = right_env.reshape(terms * width, ncol)
+        right = jnp.swapaxes(right_env, 1, 2).reshape(terms * ncol, width)
         rshape = (nl, terms * ncol, width)
     else:
         right = lax.all_gather(right_env, "lsec", axis=2, tiled=True)
@@ -304,7 +339,7 @@
         out_shape=(
             jax.ShapeDtypeStruct((width, width), BF16),
             jax.ShapeDtypeStruct((width, width), BF16),
-            jax.ShapeDtypeStruct((8, 128), F32),
+            jax.ShapeDtypeStruct((2, 2), F32),
         ),
         in_specs=[smem] * 3 + [vmem] * 3,
         out_specs=(vmem, vmem, vmem),
@@ -320,12 +355,12 @@
             pltpu.VMEM((3, 8, 128), F32),
             pltpu.VMEM((3, nr, 8, 128), F32),
             pltpu.VMEM((3, nl, 8, 128), F32),
-            dma((3, nr)),
-            dma((nr,)),
-            dma((3, nl)),
-            dma((nl,)),
-            dma((2, 9)),
-            dma((2, 9)),
+            dma((3, 2, nr)),
+            dma((2, nr)),
+            dma((4, 2, nl)),
+            dma((2, nl)),
+            dma((2, 2, 9)),
+            dma((2, 2, 9)),
             dma((3, nr)),
             dma((3, nr)),
             dma((3, nl)),
@@ -337,8 +372,8 @@
         cost_estimate=pl.CostEstimate(
             flops=8 * terms * width**3, bytes_accessed=4 * 2**20, transcendentals=2
         ),
-    )(term_shift, left_dims, right_dims, psi, left, right)
-    return image1, image2, proj[:2, :2]
+    )(term_shift.T, left_dims, right_dims, psi, left, right)
+    return image1, image2, proj
 
 
 def solution(mesh):

time: 59.7 us -> 62.3 us (1.044)
  local copies, waits for them, and re-layouts: 4.01 us -> 5.37 us
  Pallas kernels: 53.5 us -> 54.8 us
    unnamed x10 -> x11, local copies, waits for them, and re-layouts: 3.44 us -> 5.37 us
    pallas_call x1, Pallas kernels: 53.5 us -> 54.8 us  [on_device(): pl.pallas_call(functools.partial(kernel, nl, nr, gather_right, terms), ou...]
where the time goes in v2:
time: 62.3 us; the launch traced here: 62.1 us
  Pallas kernels  54.8 us (88%)
  local copies, waits for them, and re-layouts  5.37 us (9%)
  between operations  1.94 us (3%)
    pallas_call x1, Pallas kernels, on_device(): pl.pallas_call(functools.partial(kernel, nl, nr, gather_right, terms), ou...  54.8 us
    unnamed x11, local copies, waits for them, and re-layouts  5.37 us

profile of v2, /device:TPU:0, one launch (start us, length us, event | category | flops | bytes accessed | tf_op | source)
XLA Modules:
  0.0 62.1 jit_solution(1038128019356476924)
XLA Ops:
  1.9 0.0 copy-start.3
  1.9 0.7 %copy-done.3 = s32[12,2]{0,1:T(2,128)S(1)} copy-done((s32[12,2]{0,1:T(2,128)S(1)}, s32[12,2]{0,1:T(2,128)}, u32[]{:S(2)}) %copy-start.3) | copy-done | bytes 120
  2.6 0.0 copy-start
  2.6 1.0 %copy-done = bf16[12,64,256]{2,1,0:T(8,128)(2,1)S(1)} copy-done((bf16[12,64,256]{2,1,0:T(8,128)(2,1)S(1)}, bf16[12,64,256]{2,1,0:T(8,128)(2,1)}, u32[]{:S(2)}) %copy-start) | copy-done | bytes 393240
  3.6 0.0 copy-start.1
  3.6 0.9 %copy-done.1 = bf16[12,256,32]{1,2,0:T(8,128)(2,1)S(1)} copy-done((bf16[12,256,32]{1,2,0:T(8,128)(2,1)S(1)}, bf16[12,256,32]{1,2,0:T(8,128)(2,1)}, u32[]{:S(2)}) %copy-start.1) | copy-done | bytes 196632
  4.5 0.0 copy-start.2
  4.5 0.9 %copy-done.2 = bf16[256,256]{1,0:T(8,128)(2,1)S(1)} copy-done((bf16[256,256]{1,0:T(8,128)(2,1)S(1)}, bf16[256,256]{1,0:T(8,128)(2,1)}, u32[]{:S(2)}) %copy-start.2) | copy-done | bytes 131096
  5.4 54.8 %shard_map.85 = (bf16[256,256]{1,0:T(8,128)(2,1)S(1)}, bf16[256,256]{1,0:T(8,128)(2,1)S(1)}, f32[2,2]{1,0:T(2,128)S(1)}) custom-call(s32[2,12]{1,0:T(2,128)S(1)} %bitcast.7, s32[1]{0:T(128)S(6)} %copy.12.ldim_ref, s32[1]{0:T(128)S(6)} %copy.13.rdim_ref, bf16[256,256]{1,0:T(8,128)(2,1)S(1)} %copy-done.2, bf16[768,256]{1,0:T(8,128)(2,1)S(1)} %bitcast.5, ...), custom_call_target="tpu_custom_call" | custom-call | flops 1610612736 | bytes 4194304 | tf_op jit(solution)/shard_map/pallas_call | solution.py:337
  60.2 0.7 %copy.14 = bf16[256,256]{1,0:T(8,128)(2,1)} copy(bf16[256,256]{1,0:T(8,128)(2,1)S(1)} %get-tuple-element.6) | data formatting | bytes 262144
  60.9 0.7 %copy.15 = bf16[256,256]{1,0:T(8,128)(2,1)} copy(bf16[256,256]{1,0:T(8,128)(2,1)S(1)} %get-tuple-element.7) | data formatting | bytes 262144
  61.5 0.6 copy.16
Async XLA Ops:
  1.9 0.7 %copy-start.3 = (s32[12,2]{0,1:T(2,128)S(1)}, s32[12,2]{0,1:T(2,128)}, u32[]{:S(2)}) copy-start(s32[12,2]{0,1:T(2,128)} %param.11) | copy-start | bytes 292
  2.6 1.0 %copy-start = (bf16[12,64,256]{2,1,0:T(8,128)(2,1)S(1)}, bf16[12,64,256]{2,1,0:T(8,128)(2,1)}, u32[]{:S(2)}) copy-start(bf16[12,64,256]{2,1,0:T(8,128)(2,1)} %param.7) | copy-start | bytes 1179652
  3.6 0.9 %copy-start.1 = (bf16[12,256,32]{1,2,0:T(8,128)(2,1)S(1)}, bf16[12,256,32]{1,2,0:T(8,128)(2,1)}, u32[]{:S(2)}) copy-start(bf16[12,256,32]{1,2,0:T(8,128)(2,1)} %param.8) | copy-start | bytes 589828
  4.5 0.9 %copy-start.2 = (bf16[256,256]{1,0:T(8,128)(2,1)S(1)}, bf16[256,256]{1,0:T(8,128)(2,1)}, u32[]{:S(2)}) copy-start(bf16[256,256]{1,0:T(8,128)(2,1)} %psi_ref.1) | copy-start | bytes 393220

commit v3 on v2

--- a/solution.py
+++ b/solution.py
@@ -16,15 +16,22 @@
 
 def kernel(
     nl, nr, gather_right, terms,
-    shift_ref, ldim_ref, rdim_ref, psi_ref, left_ref, right_ref,
+    shift_ref, ldim_ref, rdim_ref, psi_hbm, left_hbm, right_hbm,
     image1_ref, image2_ref, proj_ref,
-    live, first, images, inner, lbuf, rbuf, w1_ref, part, row_sum, row_slots, col_slots,
-    l_send, l_recv, r_send, r_recv, h_send, h_recv, ar_send, ar_recv, ac_send, ac_recv,
+    psi_ref, live, first, images, inner, lbuf, rbuf, w1_ref, part, row_sum, row_slots, col_slots,
+    l_send, l_recv, r_send, r_recv, h_send, h_recv, ar_send, ar_recv, ac_send, ac_recv, own_sem,
 ):
-    width = psi_ref.shape[0]
+    width = psi_hbm.shape[0]
     count = float(nl * nr * width * width)
     li, ri = lax.axis_index("lsec"), lax.axis_index("rsec")
     pending = []
+    own = [
+        pltpu.make_async_copy(psi_hbm, psi_ref, own_sem.at[0]),
+        pltpu.make_async_copy(left_hbm, lbuf.at[ri], own_sem.at[1]),
+        pltpu.make_async_copy(right_hbm, rbuf.at[li] if gather_right else rbuf, own_sem.at[2]),
+    ]
+    for copy in own:
+        copy.start()
 
     def when(cond, fn):
         if cond is None:
@@ -47,6 +54,11 @@
         )
         when(cond, copy.wait_recv)
 
+    def drain(n):
+        for copy, cond in pending[:n]:
+            when(cond, copy.wait_send)
+        del pending[:n]
+
     barrier = pltpu.get_barrier_semaphore()
 
     def greet_col(i, _):
@@ -75,15 +87,12 @@
             out = out + total[:, at:at + 128]
         return out
 
+    own[0].wait()
     live32 = psi_ref[...].astype(F32) * mask
     live[4] = live32.astype(BF16)
     part[...] = jnp.zeros_like(part)
     part[0, 0:1, :] = lanes(live32 * live32)
 
-    lbuf[pl.ds(ri, 1)] = left_ref[...][None]
-    if gather_right:
-        ncol = right_ref.shape[0] // terms
-        rbuf[pl.ds(li, 1)] = right_ref[...][None]
 
     for store in (live, images):
         for k in range(9):
@@ -124,20 +133,21 @@
             total = total + col_slots[t, i]
         return jnp.sum(total, axis=1, keepdims=True)
 
-    def gather(buf, n, me, device, send_sem, recv_sem, balance):
+    def gather(mine, buf, n, me, device, send_sem, recv_sem, parts, balance):
         outer = n // 2
         o, i = me // 2, lax.rem(me, 2)
         pair = me + 1 - 2 * i
         pair_dev = device(pair)
-        balance = balance and outer > 2 and outer % 2 == 0
+        balance = balance and parts == 2 and outer > 2 and outer % 2 == 0
         mate = o + 1 - 2 * lax.rem(o, 2)
-        half = buf.shape[1] // 2
+        size = buf.shape[1] // parts
 
         def piece(at, h):
-            return buf.at[at, pl.ds(h * half, half)]
-
-        def put(at, h, sem, dev, cond):
-            send(piece(at, h), piece(at, h), sem, recv_sem.at[h, at], dev, cond)
+            return buf.at[at, pl.ds(h * size, size)]
+
+        def put(at, h, sem, dev, cond, src=None):
+            src = piece(at, h) if src is None else src
+            send(src, piece(at, h), sem, recv_sem.at[h, at], dev, cond)
 
         def got(at, h, cond=None):
             arrive(piece(at, h), send_sem.at[2, h, 0], recv_sem.at[h, at], pair_dev, cond)
@@ -147,33 +157,34 @@
                 cond = (slot != mate) if cond is None else cond & (slot != mate)
             put(slot * 2 + i, h, send_sem.at[2, h, slot], pair_dev, cond)
 
-        for h in range(2):
-            forward(o, h)
+        for h in range(parts):
+            put(me, h, send_sem.at[2, h, o], pair_dev, None, mine.at[pl.ds(h * size, size)])
         for s in range(outer - 1):
             low, high = o - s, o + s
             up = device(jnp.minimum(me + 2, n - 1))
             down = device(jnp.maximum(me - 2, 0))
-            for h in range(2):
+            for h in range(parts):
+                src = mine.at[pl.ds(h * size, size)] if s == 0 else None
                 put(jnp.maximum(low, 0) * 2 + i, h, send_sem.at[0, h, s], up,
-                    (low >= 0) & (o < outer - 1))
+                    (low >= 0) & (o < outer - 1), src)
                 put(jnp.minimum(high, outer - 1) * 2 + i, h, send_sem.at[1, h, s], down,
-                    (high < outer) & (o > 0))
+                    (high < outer) & (o > 0), src)
             if balance and s == 1:
                 got(o * 2 + 1 - i, 1)
                 put(o * 2 + 1 - i, 1, send_sem.at[3, 0, 0], device(mate * 2 + i), None)
             yield
-            for h in range(2):
+            for h in range(parts):
                 for slot, cond in ((low - 1, low - 1 >= 0), (high + 1, high + 1 < outer)):
                     slot = jnp.clip(slot, 0, outer - 1)
                     got(slot * 2 + i, h, cond)
                     forward(slot, h, cond)
         yield
         for slot in range(outer):
-            for h in range(2):
+            for h in range(parts):
                 early = balance and h == 1
                 got(slot * 2 + 1 - i, h, (slot != o) if early else None)
 
-    def halo(buf, t):
+    def halo(buf, t, chunks):
         outer = nl // 2
         o, i = li // 2, lax.rem(li, 2)
         from_pair, from_line = 1 + 6 * i, 7 - 6 * i
@@ -182,10 +193,10 @@
         goes = ((i == 0) & (o < outer - 1)) | ((i == 1) & (o > 0))
         comes = ((i == 0) & (o > 0)) | ((i == 1) & (o < outer - 1))
         east, west = (li, jnp.minimum(ri + 1, nr - 1)), (li, jnp.maximum(ri - 1, 0))
-        half = width // 2
+        size = width // chunks
 
         def piece(k, c):
-            return buf.at[k, pl.ds(c * half, half)]
+            return buf.at[k, pl.ds(c * size, size)]
 
         def put(src, dst, c, sem, dev, cond=None):
             send(piece(src, c), piece(dst, c), h_send.at[t, c, sem], h_recv.at[t, c, dst], dev, cond)
@@ -199,53 +210,57 @@
             go = ri > 0
             put(k, k - 1, c, k - 1, west, go if cond is None else go & cond)
 
-        for c in range(2):
+        for c in range(chunks):
             put(4, from_line, c, 4, pair)
             sideways(4, c, None)
             yield
-        for c in range(2):
+        for c in range(chunks):
             got(from_pair, c)
             put(from_pair, from_line, c, from_pair, onward, goes)
             sideways(from_pair, c, None)
         yield
-        for c in range(2):
+        for c in range(chunks):
             got(from_line, c, comes)
             sideways(from_line, c, comes)
         yield
-        for c in range(2):
+        for c in range(chunks):
             for k, l_ok in ((4, None), (from_pair, None), (from_line, comes)):
                 for at, r_ok in ((k + 1, ri > 0), (k - 1, ri < nr - 1)):
                     got(at, c, r_ok if l_ok is None else r_ok & l_ok)
 
     def apply_left(vec):
-        for w in range(terms):
+        def term(w, _):
             k = (shift_ref[0, w] + 1) * 3 + shift_ref[1, w] + 1
-            mine = lbuf.shape[1] // terms
-            a = lbuf[:, w * mine:(w + 1) * mine, :].reshape(width, width)
-            product = jnp.dot(a, vec[k], preferred_element_type=F32)
+            product = jnp.dot(
+                lbuf[:, w].reshape(width, width), vec[k], preferred_element_type=F32
+            )
             inner[w] = product.astype(BF16)
+            return 0
+
+        lax.fori_loop(0, terms, term, 0, unroll=2)
 
     def apply_right(c):
         half = width // 2
         at = slice(c * half, (c + 1) * half)
-        total = jnp.zeros((half, width), F32)
-        for w in range(terms):
+
+        def term(w, total):
             if gather_right:
-                b = rbuf[:, w * ncol:(w + 1) * ncol, :].reshape(width, width)
-                total = total + lax.dot_general(inner[w, at], b, NT, preferred_element_type=F32)
+                b, dims = rbuf[:, w].reshape(width, width), NT
             else:
-                total = total + lax.dot_general(
-                    inner[w, at], right_ref[w], NN, preferred_element_type=F32
-                )
+                b, dims = rbuf[w], NN
+            return total + lax.dot_general(inner[w, at], b, dims, preferred_element_type=F32)
+
+        total = lax.fori_loop(0, terms, term, jnp.zeros((half, width), F32), unroll=2)
         return total * mask[at]
 
     reduce_start(0)
-    halo1 = halo(live, 0)
+    halo1 = halo(live, 0, 1)
     next(halo1)
-    next(halo1)
-    gathers = [gather(lbuf, nr, ri, lambda r: (li, r), l_send, l_recv, False)]
+    gathers = [gather(left_hbm, lbuf, nr, ri, lambda r: (li, r), l_send, l_recv, 1, False)]
     if gather_right:
-        gathers.append(gather(rbuf, nl, li, lambda l: (l, ri), r_send, r_recv, True))
+        gathers.append(
+            gather(right_hbm, rbuf, nl, li, lambda l: (l, ri), r_send, r_recv, 2, True)
+        )
     for g in gathers:
         next(g)
     reduce_middle(0)
@@ -264,12 +279,15 @@
         first[k] = (live[k].astype(F32) * scale).astype(BF16)
     for _ in gathers[0]:
         pass
+    own[1].wait()
     apply_left(first)
+    own[2].wait()
     for g in gathers[1:]:
         for _ in g:
             pass
     half = width // 2
-    halo2 = halo(images, 1)
+    early = len(pending)
+    halo2 = halo(images, 1, 2)
     for c in range(2):
         at = slice(c * half, (c + 1) * half)
         w1 = apply_right(c)
@@ -286,6 +304,8 @@
     reduce_start(1)
     next(halo2)
     reduce_middle(1)
+    next(halo2)
+    drain(early)
     for _ in halo2:
         pass
     apply_left(images)
@@ -314,8 +334,7 @@
     bottom = jnp.where(c8 == 0, sums[1:2], sums[2:3])
     proj_ref[...] = jnp.where(r8 == 0, top, bottom)[:2, :2]
 
-    for copy, cond in pending:
-        when(cond, copy.wait_send)
+    drain(len(pending))
 
 
 def on_device(nl, nr, psi, left_env, right_env, left_dims, right_dims, term_shift):
@@ -324,14 +343,14 @@
     mine = left_env.shape[1]
     ncol = right_env.shape[2]
     gather_right = ncol % 16 == 0
-    left = left_env.reshape(terms * mine, width)
     if gather_right:
-        right = jnp.swapaxes(right_env, 1, 2).reshape(terms * ncol, width)
-        rshape = (nl, terms * ncol, width)
+        right = jnp.swapaxes(right_env, 1, 2)
+        rshape = (nl, terms, ncol, width)
     else:
         right = lax.all_gather(right_env, "lsec", axis=2, tiled=True)
-        rshape = (1, 16, 128)
+        rshape = (terms, width, width)
     vmem = pl.BlockSpec(memory_space=pltpu.VMEM)
+    hbm = pl.BlockSpec(memory_space=pl.ANY)
     smem = pl.BlockSpec(memory_space=pltpu.SMEM)
     dma = pltpu.SemaphoreType.DMA
     image1, image2, proj = pl.pallas_call(
@@ -341,14 +360,15 @@
             jax.ShapeDtypeStruct((width, width), BF16),
             jax.ShapeDtypeStruct((2, 2), F32),
         ),
-        in_specs=[smem] * 3 + [vmem] * 3,
+        in_specs=[smem] * 3 + [hbm] * 3,
         out_specs=(vmem, vmem, vmem),
         scratch_shapes=[
+            pltpu.VMEM((width, width), BF16),
             pltpu.VMEM((9, width, width), BF16),
             pltpu.VMEM((9, width, width), BF16),
             pltpu.VMEM((9, width, width), BF16),
             pltpu.VMEM((terms, width, width), BF16),
-            pltpu.VMEM((nr, terms * mine, width), BF16),
+            pltpu.VMEM((nr, terms, mine, width), BF16),
             pltpu.VMEM(rshape, BF16),
             pltpu.VMEM((width, width), F32),
             pltpu.VMEM((3, 8, 128), F32),
@@ -365,14 +385,15 @@
             dma((3, nr)),
             dma((3, nl)),
             dma((3, nl)),
+            dma((3,)),
         ],
         compiler_params=pltpu.CompilerParams(
-            collective_id=0, has_side_effects=True, vmem_limit_bytes=40 * 1024 * 1024
+            collective_id=0, has_side_effects=True, vmem_limit_bytes=56 * 1024 * 1024
         ),
         cost_estimate=pl.CostEstimate(
             flops=8 * terms * width**3, bytes_accessed=4 * 2**20, transcendentals=2
         ),
-    )(term_shift.T, left_dims, right_dims, psi, left, right)
+    )(term_shift.T, left_dims, right_dims, psi, left_env, right)
     return image1, image2, proj
 
 

time: 62.3 us -> 63.4 us (1.018)
  Pallas kernels: 54.8 us -> 58.4 us
  local copies, waits for them, and re-layouts: 5.37 us -> 2.84 us
    pallas_call x1, Pallas kernels: 54.8 us -> 58.4 us  [on_device(): pl.pallas_call(functools.partial(kernel, nl, nr, gather_right, terms), ou...]
    unnamed x11 -> x7, local copies, waits for them, and re-layouts: 5.37 us -> 2.84 us
where the time goes in v3:
time: 63.4 us; the launch traced here: 63.2 us
  Pallas kernels  58.4 us (92%)
  local copies, waits for them, and re-layouts  2.84 us (4%)
  between operations  1.94 us (3%)
    pallas_call x1, Pallas kernels, on_device(): pl.pallas_call(functools.partial(kernel, nl, nr, gather_right, terms), ou...  58.4 us
    unnamed x7, local copies, waits for them, and re-layouts  2.84 us

profile of v3, /device:TPU:0, one launch (start us, length us, event | category | flops | bytes accessed | tf_op | source)
XLA Modules:
  0.0 63.2 jit_solution(18201824009149689670)
XLA Ops:
  1.9 58.4 %shard_map.85 = (bf16[256,256]{1,0:T(8,128)(2,1)}, bf16[256,256]{1,0:T(8,128)(2,1)}, f32[2,2]{1,0:T(2,128)}) custom-call(s32[2,12]{1,0:T(2,128)} %bitcast.3, s32[1]{0:T(128)S(6)} %copy.12.ldim_ref, s32[1]{0:T(128)S(6)} %copy.13.rdim_ref, bf16[256,256]{1,0:T(8,128)(2,1)} %psi_hbm.1, bf16[12,64,256]{2,1,0:T(8,128)(2,1)} %left_hbm.1, bf16[12,32,256]{2,1,0:T(8,128)(2,1)} %bitcast.2), custom_call_target="tpu_custom_call" | custom-call | flops 1610612736 | bytes 4194304 | tf_op jit(solution)/shard_map/pallas_call | solution.py:356
  60.3 0.0 copy-start
  60.4 1.6 %copy.14 = bf16[256,256]{1,0:T(8,128)(2,1)} copy(bf16[256,256]{1,0:T(8,128)(2,1)} %get-tuple-element.6) | data formatting | bytes 262144
  62.0 0.0 copy-done
  62.0 0.0 copy-start.1
  62.0 0.7 %copy.15 = bf16[256,256]{1,0:T(8,128)(2,1)} copy(bf16[256,256]{1,0:T(8,128)(2,1)S(1)} %copy-done) | data formatting | bytes 262144
  62.6 0.0 copy-done.1
  62.6 0.6 copy.16
Async XLA Ops:
  60.3 1.6 %copy-start = (bf16[256,256]{1,0:T(8,128)(2,1)S(1)}, bf16[256,256]{1,0:T(8,128)(2,1)}, u32[]{:S(2)}) copy-start(bf16[256,256]{1,0:T(8,128)(2,1)} %get-tuple-element.7) | copy-start | bytes 393220
  62.0 0.7 %copy-start.1 = (f32[2,2]{1,0:T(2,128)S(1)}, f32[2,2]{1,0:T(2,128)}, u32[]{:S(2)}) copy-start(f32[2,2]{1,0:T(2,128)} %get-tuple-element.8) | copy-start | bytes 52

commit v4 on v3

--- a/solution.py
+++ b/solution.py
@@ -157,8 +157,6 @@
                 cond = (slot != mate) if cond is None else cond & (slot != mate)
             put(slot * 2 + i, h, send_sem.at[2, h, slot], pair_dev, cond)
 
-        for h in range(parts):
-            put(me, h, send_sem.at[2, h, o], pair_dev, None, mine.at[pl.ds(h * size, size)])
         for s in range(outer - 1):
             low, high = o - s, o + s
             up = device(jnp.minimum(me + 2, n - 1))
@@ -169,6 +167,9 @@
                     (low >= 0) & (o < outer - 1), src)
                 put(jnp.minimum(high, outer - 1) * 2 + i, h, send_sem.at[1, h, s], down,
                     (high < outer) & (o > 0), src)
+            if s == 0:
+                for h in range(parts):
+                    put(me, h, send_sem.at[2, h, o], pair_dev, None, mine.at[pl.ds(h * size, size)])
             if balance and s == 1:
                 got(o * 2 + 1 - i, 1)
                 put(o * 2 + 1 - i, 1, send_sem.at[3, 0, 0], device(mate * 2 + i), None)
@@ -254,37 +255,34 @@
         return total * mask[at]
 
     reduce_start(0)
+    left = gather(left_hbm, lbuf, nr, ri, lambda r: (li, r), l_send, l_recv, 1, False)
+    right = iter(())
+    if gather_right:
+        right = gather(right_hbm, rbuf, nl, li, lambda l: (l, ri), r_send, r_recv, 2, True)
     halo1 = halo(live, 0, 1)
+    next(right, None)
     next(halo1)
-    gathers = [gather(left_hbm, lbuf, nr, ri, lambda r: (li, r), l_send, l_recv, 1, False)]
-    if gather_right:
-        gathers.append(
-            gather(right_hbm, rbuf, nl, li, lambda l: (l, ri), r_send, r_recv, 2, True)
-        )
-    for g in gathers:
-        next(g)
+    next(left)
+    next(right, None)
+    next(halo1)
     reduce_middle(0)
+    next(left, None)
+    next(right, None)
     next(halo1)
-    steps = [nr // 2 - 1, nl // 2 - 1][:len(gathers)]
-    for s in range(max(steps)):
-        for g, n in zip(gathers, steps):
-            if s < n:
-                next(g)
-        if s == 0:
-            next(halo1)
+    for _ in range(nl // 2 - 3):
+        next(right, None)
     for _ in halo1:
         pass
     scale = lax.rsqrt(reduce_end(0)[0:1] / count + 1e-06)
     for k in range(9):
         first[k] = (live[k].astype(F32) * scale).astype(BF16)
-    for _ in gathers[0]:
+    for _ in left:
         pass
     own[1].wait()
     apply_left(first)
     own[2].wait()
-    for g in gathers[1:]:
-        for _ in g:
-            pass
+    for _ in right:
+        pass
     half = width // 2
     early = len(pending)
     halo2 = halo(images, 1, 2)
@@ -350,7 +348,7 @@
         right = lax.all_gather(right_env, "lsec", axis=2, tiled=True)
         rshape = (terms, width, width)
     vmem = pl.BlockSpec(memory_space=pltpu.VMEM)
-    hbm = pl.BlockSpec(memory_space=pl.ANY)
+    hbm = pl.BlockSpec(memory_space=pltpu.HBM)
     smem = pl.BlockSpec(memory_space=pltpu.SMEM)
     dma = pltpu.SemaphoreType.DMA
     image1, image2, proj = pl.pallas_call(
@@ -388,7 +386,7 @@
             dma((3,)),
         ],
         compiler_params=pltpu.CompilerParams(
-            collective_id=0, has_side_effects=True, vmem_limit_bytes=56 * 1024 * 1024
+            collective_id=0, has_side_effects=True, vmem_limit_bytes=32 * 1024 * 1024
         ),
         cost_estimate=pl.CostEstimate(
             flops=8 * terms * width**3, bytes_accessed=4 * 2**20, transcendentals=2

time: 63.4 us -> 62.8 us (level)
  Pallas kernels: 58.4 us -> 55.3 us
  local copies, waits for them, and re-layouts: 2.84 us -> 5.37 us
    pallas_call x1, Pallas kernels: 58.4 us -> 55.3 us  [on_device(): pl.pallas_call(functools.partial(kernel, nl, nr, gather_right, terms), ou...]
    unnamed x7 -> x11, local copies, waits for them, and re-layouts: 2.84 us -> 5.37 us
where the time goes in v4:
time: 62.8 us; the launch traced here: 62.6 us
  Pallas kernels  55.3 us (88%)
  local copies, waits for them, and re-layouts  5.37 us (9%)
  between operations  1.94 us (3%)
    pallas_call x1, Pallas kernels, on_device(): pl.pallas_call(functools.partial(kernel, nl, nr, gather_right, terms), ou...  55.3 us
    unnamed x11, local copies, waits for them, and re-layouts  5.37 us

profile of v4, /device:TPU:0, one launch (start us, length us, event | category | flops | bytes accessed | tf_op | source)
XLA Modules:
  0.0 62.6 jit_solution(1967778710754814313)
XLA Ops:
  1.9 0.0 copy-start.3
  1.9 0.7 %copy-done.3 = s32[12,2]{0,1:T(2,128)S(1)} copy-done((s32[12,2]{0,1:T(2,128)S(1)}, s32[12,2]{0,1:T(2,128)}, u32[]{:S(2)}) %copy-start.3) | copy-done | bytes 120
  2.6 0.0 copy-start
  2.6 1.0 %copy-done = bf16[12,64,256]{2,1,0:T(8,128)(2,1)S(1)} copy-done((bf16[12,64,256]{2,1,0:T(8,128)(2,1)S(1)}, bf16[12,64,256]{2,1,0:T(8,128)(2,1)}, u32[]{:S(2)}) %copy-start) | copy-done | bytes 393240
  3.6 0.0 copy-start.1
  3.6 0.9 %copy-done.1 = bf16[12,256,32]{1,2,0:T(8,128)(2,1)S(1)} copy-done((bf16[12,256,32]{1,2,0:T(8,128)(2,1)S(1)}, bf16[12,256,32]{1,2,0:T(8,128)(2,1)}, u32[]{:S(2)}) %copy-start.1) | copy-done | bytes 196632
  4.5 0.0 copy-start.2
  4.5 0.9 %copy-done.2 = bf16[256,256]{1,0:T(8,128)(2,1)S(1)} copy-done((bf16[256,256]{1,0:T(8,128)(2,1)S(1)}, bf16[256,256]{1,0:T(8,128)(2,1)}, u32[]{:S(2)}) %copy-start.2) | copy-done | bytes 131096
  5.4 55.3 %shard_map.85 = (bf16[256,256]{1,0:T(8,128)(2,1)S(1)}, bf16[256,256]{1,0:T(8,128)(2,1)S(1)}, f32[2,2]{1,0:T(2,128)S(1)}) custom-call(s32[2,12]{1,0:T(2,128)S(1)} %bitcast.3, s32[1]{0:T(128)S(6)} %copy.12.ldim_ref, s32[1]{0:T(128)S(6)} %copy.13.rdim_ref, bf16[256,256]{1,0:T(8,128)(2,1)S(1)} %copy-done.2, bf16[12,64,256]{2,1,0:T(8,128)(2,1)S(1)} %copy-done, ...), custom_call_target="tpu_custom_call" | custom-call | flops 1610612736 | bytes 4194304 | tf_op jit(solution)/shard_map/pallas_call | solution.py:354
  60.7 0.7 %copy.14 = bf16[256,256]{1,0:T(8,128)(2,1)} copy(bf16[256,256]{1,0:T(8,128)(2,1)S(1)} %get-tuple-element.6) | data formatting | bytes 262144
  61.4 0.7 %copy.15 = bf16[256,256]{1,0:T(8,128)(2,1)} copy(bf16[256,256]{1,0:T(8,128)(2,1)S(1)} %get-tuple-element.7) | data formatting | bytes 262144
  62.0 0.6 copy.16
Async XLA Ops:
  1.9 0.7 %copy-start.3 = (s32[12,2]{0,1:T(2,128)S(1)}, s32[12,2]{0,1:T(2,128)}, u32[]{:S(2)}) copy-start(s32[12,2]{0,1:T(2,128)} %param.11) | copy-start | bytes 292
  2.6 1.0 %copy-start = (bf16[12,64,256]{2,1,0:T(8,128)(2,1)S(1)}, bf16[12,64,256]{2,1,0:T(8,128)(2,1)}, u32[]{:S(2)}) copy-start(bf16[12,64,256]{2,1,0:T(8,128)(2,1)} %left_hbm.1) | copy-start | bytes 1179652
  3.6 0.9 %copy-start.1 = (bf16[12,256,32]{1,2,0:T(8,128)(2,1)S(1)}, bf16[12,256,32]{1,2,0:T(8,128)(2,1)}, u32[]{:S(2)}) copy-start(bf16[12,256,32]{1,2,0:T(8,128)(2,1)} %param.8) | copy-start | bytes 589828
  4.5 0.9 %copy-start.2 = (bf16[256,256]{1,0:T(8,128)(2,1)S(1)}, bf16[256,256]{1,0:T(8,128)(2,1)}, u32[]{:S(2)}) copy-start(bf16[256,256]{1,0:T(8,128)(2,1)} %psi_hbm.1) | copy-start | bytes 393220

commit v5 on v4

--- a/solution.py
+++ b/solution.py
@@ -238,10 +238,10 @@
             inner[w] = product.astype(BF16)
             return 0
 
-        lax.fori_loop(0, terms, term, 0, unroll=2)
+        lax.fori_loop(0, terms, term, 0, unroll=True)
 
     def apply_right(c):
-        half = width // 2
+        half = width
         at = slice(c * half, (c + 1) * half)
 
         def term(w, total):
@@ -251,14 +251,14 @@
                 b, dims = rbuf[w], NN
             return total + lax.dot_general(inner[w, at], b, dims, preferred_element_type=F32)
 
-        total = lax.fori_loop(0, terms, term, jnp.zeros((half, width), F32), unroll=2)
+        total = lax.fori_loop(0, terms, term, jnp.zeros((half, width), F32), unroll=True)
         return total * mask[at]
 
     reduce_start(0)
     left = gather(left_hbm, lbuf, nr, ri, lambda r: (li, r), l_send, l_recv, 1, False)
     right = iter(())
     if gather_right:
-        right = gather(right_hbm, rbuf, nl, li, lambda l: (l, ri), r_send, r_recv, 2, True)
+        right = gather(right_hbm, rbuf, nl, li, lambda l: (l, ri), r_send, r_recv, 1, False)
     halo1 = halo(live, 0, 1)
     next(right, None)
     next(halo1)
@@ -283,10 +283,10 @@
     own[2].wait()
     for _ in right:
         pass
-    half = width // 2
+    half = width
     early = len(pending)
-    halo2 = halo(images, 1, 2)
-    for c in range(2):
+    halo2 = halo(images, 1, 1)
+    for c in range(1):
         at = slice(c * half, (c + 1) * half)
         w1 = apply_right(c)
         w1_ref[at] = w1
@@ -312,7 +312,7 @@
     nr_ = sums[1:2] / count - 2.0 * alpha * alpha + alpha * alpha * (sums[2:3] / count)
     factor = lax.rsqrt(jnp.maximum(nr_, 0.0) + 1e-06)
     totals = [jnp.zeros((1, 128), F32)] * 3
-    for c in range(2):
+    for c in range(1):
         at = slice(c * half, (c + 1) * half)
         w1 = w1_ref[at]
         w2 = (apply_right(c) - alpha * w1) * factor

time: 62.8 us -> 58.4 us (0.930)
  Pallas kernels: 55.3 us -> 50.9 us
    pallas_call x1, Pallas kernels: 55.3 us -> 50.9 us  [on_device(): pl.pallas_call(functools.partial(kernel, nl, nr, gather_right, terms), ou...]
where the time goes in v5:
time: 58.4 us; the launch traced here: 58.2 us
  Pallas kernels  50.9 us (87%)
  local copies, waits for them, and re-layouts  5.37 us (9%)
  between operations  1.94 us (3%)
    pallas_call x1, Pallas kernels, on_device(): pl.pallas_call(functools.partial(kernel, nl, nr, gather_right, terms), ou...  50.9 us
    unnamed x11, local copies, waits for them, and re-layouts  5.37 us

profile of v5, /device:TPU:0, one launch (start us, length us, event | category | flops | bytes accessed | tf_op | source)
XLA Modules:
  0.0 58.2 jit_solution(5945794233436758292)
XLA Ops:
  1.9 0.0 copy-start.3
  1.9 0.7 %copy-done.3 = s32[12,2]{0,1:T(2,128)S(1)} copy-done((s32[12,2]{0,1:T(2,128)S(1)}, s32[12,2]{0,1:T(2,128)}, u32[]{:S(2)}) %copy-start.3) | copy-done | bytes 120
  2.6 0.0 copy-start
  2.6 1.0 %copy-done = bf16[12,64,256]{2,1,0:T(8,128)(2,1)S(1)} copy-done((bf16[12,64,256]{2,1,0:T(8,128)(2,1)S(1)}, bf16[12,64,256]{2,1,0:T(8,128)(2,1)}, u32[]{:S(2)}) %copy-start) | copy-done | bytes 393240
  3.6 0.0 copy-start.1
  3.6 0.9 %copy-done.1 = bf16[12,256,32]{1,2,0:T(8,128)(2,1)S(1)} copy-done((bf16[12,256,32]{1,2,0:T(8,128)(2,1)S(1)}, bf16[12,256,32]{1,2,0:T(8,128)(2,1)}, u32[]{:S(2)}) %copy-start.1) | copy-done | bytes 196632
  4.5 0.0 copy-start.2
  4.5 0.9 %copy-done.2 = bf16[256,256]{1,0:T(8,128)(2,1)S(1)} copy-done((bf16[256,256]{1,0:T(8,128)(2,1)S(1)}, bf16[256,256]{1,0:T(8,128)(2,1)}, u32[]{:S(2)}) %copy-start.2) | copy-done | bytes 131096
  5.4 50.9 %shard_map.85 = (bf16[256,256]{1,0:T(8,128)(2,1)S(1)}, bf16[256,256]{1,0:T(8,128)(2,1)S(1)}, f32[2,2]{1,0:T(2,128)S(1)}) custom-call(s32[2,12]{1,0:T(2,128)S(1)} %bitcast.3, s32[1]{0:T(128)S(6)} %copy.12.ldim_ref, s32[1]{0:T(128)S(6)} %copy.13.rdim_ref, bf16[256,256]{1,0:T(8,128)(2,1)S(1)} %copy-done.2, bf16[12,64,256]{2,1,0:T(8,128)(2,1)S(1)} %copy-done, ...), custom_call_target="tpu_custom_call" | custom-call | flops 1610612736 | bytes 4194304 | tf_op jit(solution)/shard_map/pallas_call | solution.py:354
  56.3 0.7 %copy.14 = bf16[256,256]{1,0:T(8,128)(2,1)} copy(bf16[256,256]{1,0:T(8,128)(2,1)S(1)} %get-tuple-element.6) | data formatting | bytes 262144
  57.0 0.7 %copy.15 = bf16[256,256]{1,0:T(8,128)(2,1)} copy(bf16[256,256]{1,0:T(8,128)(2,1)S(1)} %get-tuple-element.7) | data formatting | bytes 262144
  57.6 0.6 copy.16
Async XLA Ops:
  1.9 0.7 %copy-start.3 = (s32[12,2]{0,1:T(2,128)S(1)}, s32[12,2]{0,1:T(2,128)}, u32[]{:S(2)}) copy-start(s32[12,2]{0,1:T(2,128)} %param.11) | copy-start | bytes 292
  2.6 1.0 %copy-start = (bf16[12,64,256]{2,1,0:T(8,128)(2,1)S(1)}, bf16[12,64,256]{2,1,0:T(8,128)(2,1)}, u32[]{:S(2)}) copy-start(bf16[12,64,256]{2,1,0:T(8,128)(2,1)} %left_hbm.1) | copy-start | bytes 1179652
  3.6 0.9 %copy-start.1 = (bf16[12,256,32]{1,2,0:T(8,128)(2,1)S(1)}, bf16[12,256,32]{1,2,0:T(8,128)(2,1)}, u32[]{:S(2)}) copy-start(bf16[12,256,32]{1,2,0:T(8,128)(2,1)} %param.8) | copy-start | bytes 589828
  4.5 0.9 %copy-start.2 = (bf16[256,256]{1,0:T(8,128)(2,1)S(1)}, bf16[256,256]{1,0:T(8,128)(2,1)}, u32[]{:S(2)}) copy-start(bf16[256,256]{1,0:T(8,128)(2,1)} %psi_hbm.1) | copy-start | bytes 393220

commit v6 on v5

--- a/solution.py
+++ b/solution.py
@@ -17,7 +17,7 @@
 def kernel(
     nl, nr, gather_right, terms,
     shift_ref, ldim_ref, rdim_ref, psi_hbm, left_hbm, right_hbm,
-    image1_ref, image2_ref, proj_ref,
+    image1_hbm, image2_hbm, proj_ref,
     psi_ref, live, first, images, inner, lbuf, rbuf, w1_ref, part, row_sum, row_slots, col_slots,
     l_send, l_recv, r_send, r_recv, h_send, h_recv, ar_send, ar_recv, ac_send, ac_recv, own_sem,
 ):
@@ -293,7 +293,8 @@
         w1_bf16 = w1.astype(BF16)
         images[4, at] = w1_bf16
         next(halo2)
-        image1_ref[at] = w1_bf16
+    image1_out = pltpu.make_async_copy(images.at[4], image1_hbm, own_sem.at[3])
+    image1_out.start()
     w1 = w1_ref[...]
     v1 = first[4].astype(F32)
     part[1, 0:1, :] = lanes(v1 * w1)
@@ -316,7 +317,7 @@
         at = slice(c * half, (c + 1) * half)
         w1 = w1_ref[at]
         w2 = (apply_right(c) - alpha * w1) * factor
-        image2_ref[at] = w2.astype(BF16)
+        psi_ref[at] = w2.astype(BF16)
         v1 = first[4, at].astype(F32)
         v2 = ((w1 - alpha * v1) * factor).astype(BF16).astype(F32)
         products = (v1 * w2, v2 * w1, v2 * w2)
@@ -324,6 +325,8 @@
     for k in range(3):
         part[2, k:k + 1, :] = totals[k]
     reduce_start(2)
+    image2_out = pltpu.make_async_copy(psi_ref, image2_hbm, own_sem.at[4])
+    image2_out.start()
     reduce_middle(2)
     sums = reduce_end(2) / count
     r8 = lax.broadcasted_iota(jnp.int32, (8, 128), 0)
@@ -332,6 +335,8 @@
     bottom = jnp.where(c8 == 0, sums[1:2], sums[2:3])
     proj_ref[...] = jnp.where(r8 == 0, top, bottom)[:2, :2]
 
+    image1_out.wait()
+    image2_out.wait()
     drain(len(pending))
 
 
@@ -348,7 +353,7 @@
         right = lax.all_gather(right_env, "lsec", axis=2, tiled=True)
         rshape = (terms, width, width)
     vmem = pl.BlockSpec(memory_space=pltpu.VMEM)
-    hbm = pl.BlockSpec(memory_space=pltpu.HBM)
+    hbm = pl.BlockSpec(memory_space=pl.ANY)
     smem = pl.BlockSpec(memory_space=pltpu.SMEM)
     dma = pltpu.SemaphoreType.DMA
     image1, image2, proj = pl.pallas_call(
@@ -359,7 +364,7 @@
             jax.ShapeDtypeStruct((2, 2), F32),
         ),
         in_specs=[smem] * 3 + [hbm] * 3,
-        out_specs=(vmem, vmem, vmem),
+        out_specs=(hbm, hbm, vmem),
         scratch_shapes=[
             pltpu.VMEM((width, width), BF16),
             pltpu.VMEM((9, width, width), BF16),
@@ -383,10 +388,10 @@
             dma((3, nr)),
             dma((3, nl)),
             dma((3, nl)),
-            dma((3,)),
+            dma((5,)),
         ],
         compiler_params=pltpu.CompilerParams(
-            collective_id=0, has_side_effects=True, vmem_limit_bytes=32 * 1024 * 1024
+            collective_id=0, has_side_effects=True, vmem_limit_bytes=56 * 1024 * 1024
         ),
         cost_estimate=pl.CostEstimate(
             flops=8 * terms * width**3, bytes_accessed=4 * 2**20, transcendentals=2

time: 58.4 us -> 55.8 us (0.955)
  local copies, waits for them, and re-layouts: 5.37 us -> 2.84 us
    unnamed x11 -> x7, local copies, waits for them, and re-layouts: 5.37 us -> 2.84 us
where the time goes in v6:
time: 55.8 us; the launch traced here: 55.6 us
  Pallas kernels  50.8 us (91%)
  local copies, waits for them, and re-layouts  2.84 us (5%)
  between operations  1.94 us (3%)
    pallas_call x1, Pallas kernels, on_device(): pl.pallas_call(functools.partial(kernel, nl, nr, gather_right, terms), ou...  50.8 us
    unnamed x7, local copies, waits for them, and re-layouts  2.84 us

profile of v6, /device:TPU:0, one launch (start us, length us, event | category | flops | bytes accessed | tf_op | source)
XLA Modules:
  0.0 55.6 jit_solution(11214095163630907020)
XLA Ops:
  1.9 50.8 %shard_map.85 = (bf16[256,256]{1,0:T(8,128)(2,1)}, bf16[256,256]{1,0:T(8,128)(2,1)}, f32[2,2]{1,0:T(2,128)}) custom-call(s32[2,12]{1,0:T(2,128)} %bitcast.3, s32[1]{0:T(128)S(6)} %copy.12.ldim_ref, s32[1]{0:T(128)S(6)} %copy.13.rdim_ref, bf16[256,256]{1,0:T(8,128)(2,1)} %psi_hbm.1, bf16[12,64,256]{2,1,0:T(8,128)(2,1)} %left_hbm.1, bf16[12,32,256]{2,1,0:T(8,128)(2,1)} %bitcast.2), custom_call_target="tpu_custom_call" | custom-call | flops 1610612736 | bytes 4194304 | tf_op jit(solution)/shard_map/pallas_call | solution.py:359
  52.7 0.0 copy-start
  52.7 1.6 %copy.14 = bf16[256,256]{1,0:T(8,128)(2,1)} copy(bf16[256,256]{1,0:T(8,128)(2,1)} %get-tuple-element.6) | data formatting | bytes 262144
  54.3 0.0 copy-done
  54.3 0.0 copy-start.1
  54.3 0.7 %copy.15 = bf16[256,256]{1,0:T(8,128)(2,1)} copy(bf16[256,256]{1,0:T(8,128)(2,1)S(1)} %copy-done) | data formatting | bytes 262144
  55.0 0.0 copy-done.1
  55.0 0.6 %copy.16 = f32[2,2]{1,0:T(2,128)} copy(f32[2,2]{1,0:T(2,128)S(1)} %copy-done.1) | data formatting | bytes 32
Async XLA Ops:
  52.7 1.6 %copy-start = (bf16[256,256]{1,0:T(8,128)(2,1)S(1)}, bf16[256,256]{1,0:T(8,128)(2,1)}, u32[]{:S(2)}) copy-start(bf16[256,256]{1,0:T(8,128)(2,1)} %get-tuple-element.7) | copy-start | bytes 393220
  54.3 0.7 %copy-start.1 = (f32[2,2]{1,0:T(2,128)S(1)}, f32[2,2]{1,0:T(2,128)}, u32[]{:S(2)}) copy-start(f32[2,2]{1,0:T(2,128)} %get-tuple-element.8) | copy-start | bytes 52

commit v7 on v6

--- a/solution.py
+++ b/solution.py
@@ -324,9 +324,12 @@
         totals = [total + lanes(product) for total, product in zip(totals, products)]
     for k in range(3):
         part[2, k:k + 1, :] = totals[k]
+    late = len(pending)
     reduce_start(2)
     image2_out = pltpu.make_async_copy(psi_ref, image2_hbm, own_sem.at[4])
     image2_out.start()
+    drain(late)
+    image1_out.wait()
     reduce_middle(2)
     sums = reduce_end(2) / count
     r8 = lax.broadcasted_iota(jnp.int32, (8, 128), 0)
@@ -335,7 +338,6 @@
     bottom = jnp.where(c8 == 0, sums[1:2], sums[2:3])
     proj_ref[...] = jnp.where(r8 == 0, top, bottom)[:2, :2]
 
-    image1_out.wait()
     image2_out.wait()
     drain(len(pending))
 

time: 55.8 us -> 55.7 us (level)
  no operation moved by 1% of the time
where the time goes in v7:
time: 55.7 us; the launch traced here: 55.5 us
  Pallas kernels  50.8 us (91%)
  local copies, waits for them, and re-layouts  2.84 us (5%)
  between operations  1.94 us (3%)
    pallas_call x1, Pallas kernels, on_device(): pl.pallas_call(functools.partial(kernel, nl, nr, gather_right, terms), ou...  50.8 us
    unnamed x7, local copies, waits for them, and re-layouts  2.84 us

profile of v7, /device:TPU:0, one launch (start us, length us, event | category | flops | bytes accessed | tf_op | source)
XLA Modules:
  0.0 55.5 jit_solution(12842961754817500706)
XLA Ops:
  1.9 50.8 %shard_map.85 = (bf16[256,256]{1,0:T(8,128)(2,1)}, bf16[256,256]{1,0:T(8,128)(2,1)}, f32[2,2]{1,0:T(2,128)}) custom-call(s32[2,12]{1,0:T(2,128)} %bitcast.3, s32[1]{0:T(128)S(6)} %copy.12.ldim_ref, s32[1]{0:T(128)S(6)} %copy.13.rdim_ref, bf16[256,256]{1,0:T(8,128)(2,1)} %psi_hbm.1, bf16[12,64,256]{2,1,0:T(8,128)(2,1)} %left_hbm.1, bf16[12,32,256]{2,1,0:T(8,128)(2,1)} %bitcast.2), custom_call_target="tpu_custom_call" | custom-call | flops 1610612736 | bytes 4194304 | tf_op jit(solution)/shard_map/pallas_call | solution.py:361
  52.7 0.0 copy-start
  52.7 1.6 %copy.14 = bf16[256,256]{1,0:T(8,128)(2,1)} copy(bf16[256,256]{1,0:T(8,128)(2,1)} %get-tuple-element.6) | data formatting | bytes 262144
  54.3 0.0 copy-done
  54.3 0.0 copy-start.1
  54.3 0.7 %copy.15 = bf16[256,256]{1,0:T(8,128)(2,1)} copy(bf16[256,256]{1,0:T(8,128)(2,1)S(1)} %copy-done) | data formatting | bytes 262144
  55.0 0.0 copy-done.1
  55.0 0.6 %copy.16 = f32[2,2]{1,0:T(2,128)} copy(f32[2,2]{1,0:T(2,128)S(1)} %copy-done.1) | data formatting | bytes 32
Async XLA Ops:
  52.7 1.6 %copy-start = (bf16[256,256]{1,0:T(8,128)(2,1)S(1)}, bf16[256,256]{1,0:T(8,128)(2,1)}, u32[]{:S(2)}) copy-start(bf16[256,256]{1,0:T(8,128)(2,1)} %get-tuple-element.7) | copy-start | bytes 393220
  54.3 0.7 %copy-start.1 = (f32[2,2]{1,0:T(2,128)S(1)}, f32[2,2]{1,0:T(2,128)}, u32[]{:S(2)}) copy-start(f32[2,2]{1,0:T(2,128)} %get-tuple-element.8) | copy-start | bytes 52
